TPU v7x, 256 devices: a whole 4x4x8 slice. The times are simulated.
256 devices in a mesh: replica: 8 (over x, core), group: 32 (over z, y).
Axes of the slice: x: 4, y: 4, z: 8, core: 2. Of those that a mesh axis runs over, the one named last changes fastest.
Arguments:
- token_values: bfloat16 [10240, 7168], P(('replica', 'group')), parts along dimension 0, may hold values from -6 to 6
- token_scales: bfloat16 [10240, 56], P(('replica', 'group')), parts along dimension 0, may hold values from 0.25 to 4
- counts: int32 [256], P('replica'), parts along dimension 0, may hold values from 1 to 40, 768 in all
- gate_values: bfloat16 [9216, 7168], P('group'), may hold values from -0.0625 to 0.0625
- gate_scales: float32 [9216, 56], P('group'), may hold values from 0.5 to 2
- up_values: bfloat16 [9216, 7168], P('group'), may hold values from -0.0625 to 0.0625
- up_scales: float32 [9216, 56], P('group'), may hold values from 0.5 to 2
- down_values: bfloat16 [9216, 3584], P('group'), may hold values from -0.0625 to 0.0625
- down_scales: float32 [9216, 28], P('group'), may hold values from 0.5 to 2
Outputs:
- mixed: bfloat16 [10240, 3584], P(('replica', 'group')), parts along dimension 0
There are 8 independent parts, one for each index of `replica`. A program takes and returns all parts, laid end to end along the dimension named above; an argument that names none is the same for every part. Nothing has to cross between parts.
Inputs may be any that keep to these rules, and one draw needn't show every extreme that they name: Device i's live tokens are its first counts[i] slots; the counts of a part sum to 768 and some device has exactly 40.
All inputs are finite; a program needn't handle non-finite values.
Results may differ from a plain program's by a relative error of at most 0.02.
Values may be sent and summed in bfloat16 or wider, within the bound.
A program may use at most 192 MiB of HBM per device.

v0:
```python
import jax
import jax.numpy as jnp
from jax import lax
from jax.sharding import PartitionSpec as P


def dequant(values, scales):
    row_count, feat_width = values.shape
    blocks = scales.shape[1]
    expanded = (
        values.astype(jnp.float32).reshape(row_count, blocks, feat_width // blocks)
        * scales.astype(jnp.float32)[:, :, None]
    )
    return expanded.reshape(row_count, feat_width).astype(jnp.bfloat16)


def lookup(table, index, groups):
    match = index[:, None] == jnp.arange(groups, dtype=jnp.int32)[None, :]
    return jnp.sum(jnp.where(match, table[None, :], 0), axis=1)


def rounded(term):
    narrow = lax.optimization_barrier(term.astype(jnp.bfloat16))
    return narrow.astype(jnp.float32)


def shards(
    token_values,
    token_scales,
    counts,
    gate_values,
    gate_scales,
    up_values,
    up_scales,
    down_values,
    down_scales,
):
    w_gate = dequant(gate_values, gate_scales)
    w_up = dequant(up_values, up_scales)
    w_down = dequant(down_values, down_scales)
    gathered_values, gathered_scales = (
        lax.all_gather(token_values, "group", axis=0, tiled=True),
        lax.all_gather(token_scales, "group", axis=0, tiled=True),
    )
    token_rows = dequant(gathered_values, gathered_scales)
    slot_count = token_values.shape[0]
    groups = lax.axis_size("group")
    slot_total = slot_count * groups
    position = jnp.arange(slot_total, dtype=jnp.int32)
    owner_of = position // slot_count
    within = position % slot_count
    live_mask = within < lookup(counts, owner_of, groups)
    contract = (((1,), (1,)), ((), ()))
    gate_act = lax.dot_general(token_rows, w_gate, contract, preferred_element_type=jnp.float32)
    up_act = lax.dot_general(token_rows, w_up, contract, preferred_element_type=jnp.float32)
    hidden = jnp.where(
        live_mask[:, None],
        (jax.nn.silu(gate_act) * up_act).astype(jnp.bfloat16),
        jnp.zeros((), jnp.bfloat16),
    )
    return lax.psum_scatter(
        rounded(jnp.dot(hidden, w_down, preferred_element_type=jnp.float32)).astype(jnp.bfloat16),
        "group",
        scatter_dimension=0,
        tiled=True,
    )


def solution(mesh):
    in_specs = (
        P(("replica", "group"), None),
        P(("replica", "group"), None),
        P("replica"),
        P("group", None),
        P("group", None),
        P("group", None),
        P("group", None),
        P("group", None),
        P("group", None),
    )
    out_specs = P(("replica", "group"), None)
    return jax.shard_map(shards, mesh=mesh, in_specs=in_specs, out_specs=out_specs, check_vma=False)
```

profile of v0, /device:TPU:4, one launch (start us, length us, event | category | flops | bytes accessed | tf_op | source)
XLA Modules:
  0.0 475.3 jit_solution(12935518796696062441)
XLA Ops:
  6.5 0.0 all-gather.2.cloned.1.call-start
  6.5 0.7 all-gather.2.cloned.1.call-update
  7.3 0.0 reduce-scatter.2.cloned.1.call-start
  7.3 1.6 copy.16
  8.9 1.7 copy.17
  10.6 0.9 copy.18
  11.5 52.8 %all_gather.7 = bf16[1280,56]{1,0:T(8,128)(2,1)S(1)} all-gather(bf16[40,56]{1,0:T(8,128)(2,1)} %param.10), channel_id=1, replica_groups=mesh['replica'=8,'group'=32] {'group'}, dimensions={0}, use_global_device_ids=true | all-gather | bytes 147840 | tf_op jit(solution)/shard_map/all_gather | solution.py:43
  64.3 0.8 select_reduce_fusion
  65.1 96.5 %all-gather.2.cloned.1.call-done = bf16[1280,7168]{1,0:T(8,128)(2,1)} async-done(((bf16[40,7168]{1,0:T(8,128)(2,1)}), bf16[1280,7168]{1,0:T(8,128)(2,1)}) %all-gather.2.cloned.1.call-update) | async-done | bytes 18350096 | tf_op jit(solution)/shard_map/all_gather | solution.py:42
  161.6 0.0 copy-start
  161.6 12.3 %mul.51 = f32[1280,56,128]{2,1,0:T(8,128)} broadcast(bf16[1280,56]{1,0:T(8,128)(2,1)S(1)} %all_gather.7), dimensions={0,1} | broadcast | bytes 36843520 | tf_op jit(solution)/shard_map/mul | solution.py:11
  173.9 0.0 copy-done
  173.9 2.3 mul.54
  176.2 23.5 %fusion.3 = f32[1280,288]{0,1:T(8,128)S(1)} fusion(f32[36,8,56,128]{3,2,1,0:T(8,128)S(1)} %bitcast.34, bf16[288,7168]{1,0:T(8,128)(2,1)} %param.12, f32[160,8,56,128]{3,2,1,0:T(8,128)} %bitcast.32, bf16[1280,7168]{1,0:T(8,128)(2,1)} %all-gather.2.cloned.1.call-done), kind=kOutput, calls=%fused_computation.7 | convolution fusion | flops 5318541312 | bytes 68911104 | tf_op jit(solution)/shard_map/dot_general | solution.py:54
  199.8 3.2 mul.58
  202.9 24.3 %fusion.14 = bf16[1280,288]{0,1:T(8,128)(2,1)} fusion(f32[36,8,56,128]{3,2,1,0:T(8,128)S(1)} %bitcast.35, bf16[288,7168]{1,0:T(8,128)(2,1)} %param.14, f32[1280,288]{0,1:T(8,128)S(1)} %fusion.3, pred[1280]{0:T(1024)(128)(4,1)S(1)} %fusion.18, f32[160,8,56,128]{3,2,1,0:T(8,128)} %bitcast.33, bf16[1280,7168]{1,0:T(8,128)(2,1)} %all-gather.2.cloned.1.call-done), kind=kOutput, calls=%fused_computation.13 | convolution fusion | flops 5321121792 | bytes 69649664 | tf_op jit(solution)/shard_map/dot_general | solution.py:55
  227.3 1.3 mul.62
  228.5 11.3 %convolution_convert_fusion = bf16[1280,3584]{1,0:T(8,128)(2,1)} fusion(bf16[1280,288]{0,1:T(8,128)(2,1)} %fusion.14, f32[36,8,28,128]{3,2,1,0:T(8,128)S(1)} %bitcast.36, bf16[288,3584]{1,0:T(8,128)(2,1)} %param.16), kind=kOutput, calls=%fused_computation.2 | convolution fusion | flops 2650095616 | bytes 16105472 | tf_op jit(solution)/shard_map/dot_general | solution.py:62
  239.8 0.0 reduce-scatter.2.cloned.1.call-update
  239.8 228.6 %reduce-scatter.2.cloned.1.call-done = bf16[40,3584]{1,0:T(8,128)(2,1)} async-done(((bf16[1280,3584]{1,0:T(8,128)(2,1)}), bf16[40,3584]{1,0:T(8,128)(2,1)}) %reduce-scatter.2.cloned.1.call-update) | async-done | bytes 286736 | tf_op jit(solution)/shard_map/reduce_scatter | solution.py:61
  (2 shorter events, 0.0 us)
Async XLA Ops:
  6.5 155.1 %all-gather.2.cloned.1.call-start = ((), (), s32[]{:S(2)}) async-start(), calls=%async_computation.1 | async-start | bytes 18923520 | tf_op jit(solution)/shard_map/all_gather | solution.py:42
  7.3 461.2 %reduce-scatter.2.cloned.1.call-start = ((), (), s32[]{:S(2)}) async-start(), calls=%async_computation.2 | async-start | bytes 9461760 | tf_op jit(solution)/shard_map/reduce_scatter | solution.py:61
  161.6 12.3 %copy-start = (f32[288,56]{1,0:T(8,128)S(1)}, f32[288,56]{1,0:T(8,128)}, u32[]{:S(2)}) copy-start(f32[288,56]{1,0:T(8,128)} %copy.16) | copy-start | bytes 193540
Sparse Core Ops, SparseCore 0:
  9.9 151.6 all-gather.1
  239.9 228.4 reduce-scatter.1
where the time goes:
time: 476 us; the launch traced here: 475 us
  waiting for transfers between devices  326 us (68%)
  matrix products  59.1 us (12%)
  blocking collectives  52.8 us (11%)
  local copies, waits for them, and re-layouts  23.2 us (5%)
  between operations  13.4 us (3%)
    reduce_scatter x1, waiting for transfers between devices, shards(): lax.psum_scatter(rounded(jnp.dot(hidden, w_down, preferred_element_type=j...  229 us
    all_gather x1, waiting for transfers between devices, shards(): lax.all_gather(token_values, 'group', axis=0, tiled=True)  96.5 us
    all_gather x1, blocking collectives, shards(): lax.all_gather(token_scales, 'group', axis=0, tiled=True)  52.8 us
    dot_general x1, matrix products, shards(): lax.dot_general(token_rows, w_up, contract, preferred_element_type=jnp.fl...  24.3 us
    dot_general x1, matrix products, shards(): lax.dot_general(token_rows, w_gate, contract, preferred_element_type=jnp....  23.5 us
    mul x4, local copies, waits for them, and re-layouts, dequant(): values.astype(jnp.float32).reshape(row_count, blocks, feat_width // blocks)  19 us
    dot_general x1, matrix products, shards(): jnp.dot(hidden, w_down, preferred_element_type=jnp.float32)  11.3 us
  transfers between devices with their start and end apart: 2, of which 2 were waited for; matrix products, arithmetic and copies ran while one was open for 1% of the time, Pallas kernels for 0%

commit v1 on v0

v1 whole, which is shorter than its diff:
```python
import jax
import jax.numpy as jnp
from jax import lax
from jax.experimental import pallas as pl
from jax.experimental.pallas import tpu as pltpu
from jax.sharding import PartitionSpec as P

F32, BF16, I32 = jnp.float32, jnp.bfloat16, jnp.int32
N, NZ, NY = 32, 8, 4
CAP, LIVE = 40, 768
D, DO, FF = 7168, 3584, 288
HOLD = 28
PW, OW = 256, 128
HALF = LIVE // 2
NSUB = 4
SUB = HALF // NSUB
STEPS = N // 2
FP = 384
T1 = 480
T2 = LIVE - T1
H1, H2 = T1 // 2, T2 // 2
OROW = 48
ORDER = (4, 3, -3, 2, -2, 1, -1, 0)


def kernel(
    counts, tv_h, ts_h, gv_h, gs_h, uv_h, us_h, dv_h, ds_h, out,
    tv, ts, gv, gs, uv, us, dv, ds, asrc, adst, xs, onehot, back, w, wd, acc, hid, ring,
    r1, r2, yz, zr, tz, ty1, ty2, res, osrc, odst,
    ld, a_s, a_r, g_s, g_r, s1, q1, s2, q2, sz, qz, st, qt, sy1, qy1, sy2, qy2, o_s, o_r,
):
    rep = lax.axis_index("replica")
    g = lax.axis_index("group")
    z, y = g // NY, g % NY
    up_y, dn_y = z * NY + (y + 1) % NY, z * NY + (y + 3) % NY
    up_z, dn_z = ((z + 1) % NZ) * NY + y, ((z + 7) % NZ) * NY + y
    is_holder = g < HOLD

    def remote(src, dst, send, recv, to):
        return pltpu.make_async_remote_copy(
            src, dst, send, recv, device_id=(rep, to), device_id_type=pl.DeviceIdType.MESH
        )

    loads = [
        pltpu.make_async_copy(a, b, ld.at[i])
        for i, (a, b) in enumerate(
            ((tv_h, tv), (ts_h, ts), (gv_h, gv), (gs_h, gs), (uv_h, uv), (us_h, us), (dv_h, dv), (ds_h, ds))
        )
    ]
    for load in loads:
        load.start()
    barrier = pltpu.get_barrier_semaphore()

    def greet(i, c):
        pl.semaphore_signal(barrier, inc=1, device_id=(rep, (g + i) % N), device_id_type=pl.DeviceIdType.MESH)
        return c

    lax.fori_loop(1, N, greet, 0)

    loads[0].wait()
    loads[1].wait()
    tsf = ts[...].astype(F32)
    for p in range(HOLD):
        lo = tv[:, PW * p : PW * p + 128].astype(F32) * tsf[:, 2 * p : 2 * p + 1]
        hi = tv[:, PW * p + 128 : PW * p + 256].astype(F32) * tsf[:, 2 * p + 1 : 2 * p + 2]
        asrc[p] = jnp.concatenate([lo, hi], axis=0).astype(BF16)
    pl.semaphore_wait(barrier, N - 1)

    def scatter(i, c):
        to = (g + i) % N

        @pl.when(to < HOLD)
        def _():
            remote(asrc.at[to], adst.at[g], a_s, a_r, to).start()

        return c

    lax.fori_loop(1, N, scatter, 0)

    offs, off = [], jnp.int32(0)
    lane = lax.broadcasted_iota(I32, (16, N * CAP), 1)
    target = jnp.full((16, N * CAP), -1, I32)
    for i in range(N):
        c = counts[i]
        rel = lane - CAP * i
        target = jnp.where((rel >= 0) & (rel < c), rel + off, target)
        offs.append(off)
        off = off + c
    row16 = lax.broadcasted_iota(I32, (16, N * CAP), 0)

    def build(r, c):
        hit = target == row16 + r * 16
        onehot[pl.ds(pl.multiple_of(r * 16, 16), 16), :] = jnp.where(hit, 1.0, 0.0).astype(BF16)
        return c

    lax.fori_loop(0, LIVE // 16, build, 0)

    for v, s, at in ((gv, gs, 0), (uv, us, FP)):
        loads[2 if at == 0 else 4].wait()
        loads[3 if at == 0 else 5].wait()

        def deq(r, c, v=v, s=s, at=at):
            r0 = pl.multiple_of(r * 32, 32)
            sf = s[pl.ds(r0, 32), :]
            for b in range(D // 128):
                val = v[pl.ds(r0, 32), 128 * b : 128 * b + 128].astype(F32) * sf[:, b : b + 1]
                w[b // 2, pl.ds(at + r0, 32), 128 * (b % 2) : 128 * (b % 2) + 128] = val.astype(BF16)
            return c

        lax.fori_loop(0, FF // 32, deq, 0)

    def pad(p, c):
        w[p, FF:FP, :] = jnp.zeros((FP - FF, PW), BF16)
        w[p, FP + FF :, :] = jnp.zeros((FP - FF, PW), BF16)
        return c

    lax.fori_loop(0, HOLD, pad, 0)
    acc[...] = jnp.zeros_like(acc)

    @pl.when(is_holder)
    def _():
        adst[g] = asrc[g]
        pltpu.make_async_copy(adst.at[pl.ds(0, N - 1)], adst.at[pl.ds(0, N - 1)], a_r).wait()

        def spread(k, c):
            a = adst[2 * k].astype(F32)
            b = adst[2 * k + 1].astype(F32)
            rows = pl.ds(pl.multiple_of(k * 80, 16), 80)
            xs[rows, 0:128] = jnp.concatenate([a[:CAP], b[:CAP]], axis=0).astype(BF16)
            xs[rows, 128:256] = jnp.concatenate([a[CAP:], b[CAP:]], axis=0).astype(BF16)
            return c

        lax.fori_loop(0, N // 2, spread, 0)

    corner = (y + z) % NY
    nxt = (
        jnp.where(corner == 3, up_z, up_y),
        jnp.where(corner == 0, dn_z, dn_y),
        jnp.where(corner == 3, up_y, up_z),
        jnp.where(corner == 0, dn_y, dn_z),
    )
    turn = (z + 32 - 3 * y) % NZ
    pos_a = NY * z + corner
    pos_b = jnp.where(turn < 4, 4 * y + turn, 4 * (y + 4) + turn - 4)

    def source(q, d):
        p = ((pos_a if q < 2 else pos_b) + (64 - d if q % 2 == 0 else d)) % N
        hi, r = p // 4, p % 4
        if q < 2:
            return hi * NY + (r + 8 - hi) % NY
        return ((3 * hi + r) % NZ) * NY + hi % NY

    def last(q, u):
        return (u < NSUB // 2) == (q % 2 == 0)

    def piece(q, u, src):
        return ring.at[src, pl.ds((q // 2) * HALF + u * SUB, SUB), :]

    def forward(q, u, src, d):
        ref = piece(q, u, src)
        return remote(ref, ref, g_s.at[q, d], g_r.at[q, u, d], nxt[q])

    def multiply(src, r0, n):
        acc[pl.ds(r0, n), :] += lax.dot_general(
            ring[src, pl.ds(r0, n), :], w[src], (((1,), (1,)), ((), ())), preferred_element_type=F32
        )

    @pl.when(is_holder)
    def _():
        for h in range(2):
            ring[g, pl.ds(h * HALF, HALF), :] = jnp.dot(
                onehot[pl.ds(h * HALF, HALF), :], xs[...], preferred_element_type=F32
            ).astype(BF16)
            for u in range(NSUB):
                for q in (2 * h, 2 * h + 1):
                    forward(q, u, g, 0).start()
        multiply(g, 0, HALF)
        multiply(g, HALF, HALF)

    loads[6].wait()
    loads[7].wait()

    def deq_down(r, c):
        r0 = pl.multiple_of(r * 32, 32)
        sf = ds[pl.ds(r0, 32), :]
        for b in range(HOLD):
            val = dv[pl.ds(r0, 32), 128 * b : 128 * b + 128].astype(F32) * sf[:, b : b + 1]
            wd[b % NY, pl.ds(r0, 32), 128 * (b // NY) : 128 * (b // NY) + 128] = val.astype(BF16)
        return c

    lax.fori_loop(0, FF // 32, deq_down, 0)
    wd[:, FF:, :] = jnp.zeros((NY, FP - FF, DO // NY), BF16)

    def gather(t, c):
        srcs = [source(q, t + 1) for q in range(4)]
        for u in range(NSUB):
            for q in range(4):

                @pl.when(srcs[q] < HOLD)
                def _(q=q, u=u):
                    forward(q, u, srcs[q], t).wait_recv()
                    if last(q, u):
                        forward(q, u, srcs[q], t + 1).start()
                    else:

                        @pl.when(t < STEPS - 2)
                        def _():
                            forward(q, u, srcs[q], t + 1).start()

        for q in range(4):

            @pl.when(srcs[q] < HOLD)
            def _(q=q):
                multiply(srcs[q], (q // 2) * HALF, HALF)

        return c

    lax.fori_loop(0, STEPS - 1, gather, 0)
    for q in range(4):
        src = source(q, STEPS)

        @pl.when(src < HOLD)
        def _(q=q, src=src):
            for u in range(NSUB):
                if last(q, u):
                    forward(q, u, src, STEPS - 1).wait_recv()
            multiply(src, (q // 2) * HALF + (q % 2) * (HALF // 2), HALF // 2)

    for r in range(LIVE // 128):
        rows = pl.ds(r * 128, 128)
        gate = acc[rows, 0:FP]
        hid[rows, :] = (gate / (1.0 + jnp.exp(-gate)) * acc[rows, FP : 2 * FP]).astype(BF16)

    def slab(dy):
        yy = (y + dy) % NY
        for r in range(4):
            rows = pl.ds(r * 192, 192)
            part = jnp.dot(hid[rows, :], wd[yy], preferred_element_type=F32).astype(BF16)
            for zp in range(7):
                w[zp * NY + yy, rows, 0:OW] = part[:, zp * OW : (zp + 1) * OW]

    def part(zp, dy, r0, n):
        return w.at[zp * NY + (y + dy) % NY, pl.ds(r0, n), 0:OW]

    def add(ref, r0, n, *others):
        total = ref[pl.ds(r0, n), :].astype(F32)
        for other in others:
            total = total + other[...].astype(F32)
        return total

    zps = [(z + dz + 8) % NZ for dz in ORDER]

    def m1(k, up):
        if up:
            return remote(part(zps[k], 2, 0, H1), r1.at[0, k], s1.at[0, k], q1.at[0, k], up_y)
        return remote(part(zps[k], 2, H1, H1), r1.at[1, k], s1.at[1, k], q1.at[1, k], dn_y)

    def m2(k, up):
        if up:
            return remote(part(zps[k], 1, 0, T1), r2.at[0, k], s2.at[0, k], q2.at[0, k], up_y)
        return remote(part(zps[k], 3, 0, T1), r2.at[1, k], s2.at[1, k], q2.at[1, k], dn_y)

    def mz(k, way, dist):
        to = up_z if way == 0 else dn_z
        if dist == 4:
            rows = pl.ds(way * H1, H1)
            return remote(yz.at[k, rows, :], zr.at[way, 3, rows, :], sz.at[way, 3], qz.at[way, 3], to)
        return remote(yz.at[k], zr.at[way, dist - 1], sz.at[way, dist - 1], qz.at[way, dist - 1], to)

    def mt(k, way, dist, yp):
        to = up_z if way == 0 else dn_z
        p = zps[k] * NY + yp
        if dist == 4:
            src = w.at[p, pl.ds(T1 + way * H2, H2), 0:OW]
            dst = tz.at[way, 3, yp, pl.ds(way * H2, H2), :]
            return remote(src, dst, st.at[way, 3, yp], qt.at[way, 3, yp], to)
        src = w.at[p, pl.ds(T1, T2), 0:OW]
        return remote(src, tz.at[way, dist - 1, yp], st.at[way, dist - 1, yp], qt.at[way, dist - 1, yp], to)

    def my1(up):
        if up:
            return remote(part(z, 2, T1, H2), ty1.at[0], sy1.at[0], qy1.at[0], up_y)
        return remote(part(z, 2, T1 + H2, H2), ty1.at[1], sy1.at[1], qy1.at[1], dn_y)

    def my2(up):
        if up:
            return remote(part(z, 1, T1, T2), ty2.at[0], sy2.at[0], qy2.at[0], up_y)
        return remote(part(z, 3, T1, T2), ty2.at[1], sy2.at[1], qy2.at[1], dn_y)

    def guarded(k, f):
        pl.when(zps[k] < 7)(f)

    def second(k):
        def f():
            for way in range(2):
                m1(k, way == 0).wait_recv()
                ref = part(zps[k], 1 if way == 0 else 3, way * H1, H1)
                ref[...] = (ref[...].astype(F32) + r1[way, k].astype(F32)).astype(BF16)
                m2(k, way == 0).start()

        guarded(k, f)

    def line(k):
        dz = ORDER[k]

        def f():
            m2(k, True).wait_recv()
            m2(k, False).wait_recv()
            ways = {4: (), 0: (0, 1)}.get(dz, (0,) if dz > 0 else (1,))
            for way in ways:
                mz(k, way, abs(dz) + 1).wait_recv()
            for h in range(2):
                rows = pl.ds(h * H1, H1)
                total = part(zps[k], 0, h * H1, H1)[...].astype(F32)
                total = total + r2[0, k, rows, :].astype(F32) + r2[1, k, rows, :].astype(F32)
                for way in ways:
                    if abs(dz) < 3 or way == h:
                        total = total + zr[way, abs(dz), rows, :].astype(F32)
                if dz == 0:
                    res[rows, :] = total.astype(BF16)
                else:
                    yz[k, rows, :] = total.astype(BF16)
            if dz == 4:
                mz(k, 0, 4).start()
                mz(k, 1, 4).start()
            elif dz != 0:
                mz(k, ways[0], abs(dz)).start()

        guarded(k, f)

    def plane(dist):
        if dist == 4:

            def f():
                for yp in range(NY):
                    mt(0, 0, 4, yp).start()
                    mt(0, 1, 4, yp).start()

            guarded(0, f)
            return
        if dist == 0:
            k = len(ORDER) - 1

            def f():
                for dy in (2, 1, 3, 0):
                    yp = (y + dy) % NY
                    mt(k, 0, 1, yp).wait_recv()
                    mt(k, 1, 1, yp).wait_recv()
                    ref = part(z, dy, T1, T2)
                    ref[...] = (ref[...].astype(F32) + tz[0, 0, yp].astype(F32) + tz[1, 0, yp].astype(F32)).astype(BF16)
                    if dy == 2:
                        my1(True).start()
                        my1(False).start()

            guarded(k, f)
            return
        for yp in range(NY):
            for way in range(2):
                k = ORDER.index(dist if way == 0 else -dist)

                def f(k=k, way=way, yp=yp):
                    mt(k, way, dist + 1, yp).wait_recv()
                    if dist == 3:
                        ref = w.at[zps[k] * NY + yp, pl.ds(T1 + way * H2, H2), 0:OW]
                        got = tz[way, 3, yp, pl.ds(way * H2, H2), :]
                    else:
                        ref = w.at[zps[k] * NY + yp, pl.ds(T1, T2), 0:OW]
                        got = tz[way, dist, yp]
                    ref[...] = (ref[...].astype(F32) + got.astype(F32)).astype(BF16)
                    mt(k, way, dist, yp).start()

                guarded(k, f)

    def cross():
        def f():
            for way in range(2):
                my1(way == 0).wait_recv()
                ref = part(z, 1 if way == 0 else 3, T1 + way * H2, H2)
                ref[...] = (ref[...].astype(F32) + ty1[way].astype(F32)).astype(BF16)
                my2(way == 0).start()

        pl.when(z < 7)(f)

    slab(2)
    for k in range(8):

        def f(k=k):
            m1(k, True).start()
            m1(k, False).start()

        guarded(k, f)
    slab(1)
    slab(3)
    slab(0)
    plane(4)
    second(0)
    second(1)
    plane(3)
    for k in range(2, 8):
        second(k)
    plane(2)
    line(0)
    plane(1)
    line(1)
    line(2)
    line(3)
    plane(0)
    line(4)
    cross()

    jrow = lax.broadcasted_iota(I32, (OROW, LIVE), 0)
    diff = lax.broadcasted_iota(I32, (OROW, LIVE), 1) - jrow
    for i in range(N):
        hit = (diff == offs[i]) & (jrow < counts[i])
        back[i * OROW : (i + 1) * OROW, :] = jnp.where(hit, 1.0, 0.0).astype(BF16)

    line(5)
    line(6)
    line(7)

    @pl.when(z < 7)
    def _():
        my2(True).wait_recv()
        my2(False).wait_recv()
        total = part(z, 0, T1, T2)[...].astype(F32) + ty2[0].astype(F32) + ty2[1].astype(F32)
        res[T1:, :] = total.astype(BF16)
        for h in range(4):
            slots = jnp.dot(back[h * 384 : (h + 1) * 384, :], res[...], preferred_element_type=F32).astype(BF16)
            for i in range(8):
                osrc[8 * h + i] = slots[i * OROW : (i + 1) * OROW]
        odst[g] = osrc[g]

        def give(i, c):
            to = (g + i) % N
            remote(osrc.at[to], odst.at[g], o_s, o_r, to).start()
            return c

        lax.fori_loop(1, N, give, 0)

    def drain(t, c):
        for q in range(4):

            @pl.when(source(q, t) < HOLD)
            def _(q=q):
                ref = ring.at[0, pl.ds(0, HALF), :]
                pltpu.make_async_copy(ref, ref, g_s.at[q, t]).wait()

        return c

    lax.fori_loop(0, STEPS - 1, drain, 0)
    for q in range(4):

        @pl.when(source(q, STEPS - 1) < HOLD)
        def _(q=q):
            ref = ring.at[0, pl.ds(0, HALF // 2), :]
            pltpu.make_async_copy(ref, ref, g_s.at[q, STEPS - 1]).wait()

    for k in range(8):

        def f(k=k):
            dz = ORDER[k]
            for way in range(2):
                m1(k, way == 0).wait_send()
                m2(k, way == 0).wait_send()
                if dz == 4 or (dz > 0 and way == 0) or (dz < 0 and way == 1):
                    mz(k, way, abs(dz)).wait_send()
                    for yp in range(NY):
                        mt(k, way, abs(dz), yp).wait_send()

        guarded(k, f)

    @pl.when(is_holder)
    def _():
        some = asrc.at[pl.ds(0, HOLD - 1)]
        pltpu.make_async_copy(some, some, a_s).wait()
        for way in range(2):
            my1(way == 0).wait_send()
            my2(way == 0).wait_send()
        some = odst.at[pl.ds(0, HOLD - 1)]
        pltpu.make_async_copy(some, some, o_r).wait()
        some = osrc.at[pl.ds(0, N - 1)]
        pltpu.make_async_copy(some, some, o_s).wait()

    @pl.when(g >= HOLD)
    def _():
        some = asrc.at[pl.ds(0, HOLD)]
        pltpu.make_async_copy(some, some, a_s).wait()
        some = odst.at[pl.ds(0, HOLD)]
        pltpu.make_async_copy(some, some, o_r).wait()

    for p in range(HOLD):
        out[:, p * OW : (p + 1) * OW] = odst[p][:CAP]


def shards(tv, ts, counts, gv, gs, uv, us, dv, ds):
    any_space = pl.BlockSpec(memory_space=pl.ANY)
    vmem, dma = pltpu.VMEM, pltpu.SemaphoreType.DMA
    return pl.pallas_call(
        kernel,
        out_shape=jax.ShapeDtypeStruct((CAP, DO), BF16),
        in_specs=[pl.BlockSpec(memory_space=pltpu.SMEM)] + [any_space] * 8,
        out_specs=pl.BlockSpec(memory_space=pltpu.VMEM),
        scratch_shapes=[
            vmem((CAP, D), BF16),
            vmem((CAP, D // 128), BF16),
            vmem((FF, D), BF16),
            vmem((FF, D // 128), F32),
            vmem((FF, D), BF16),
            vmem((FF, D // 128), F32),
            vmem((FF, DO), BF16),
            vmem((FF, DO // 128), F32),
            vmem((HOLD, 2 * CAP, 128), BF16),
            vmem((N, 2 * CAP, 128), BF16),
            vmem((N * CAP, PW), BF16),
            vmem((LIVE, N * CAP), BF16),
            vmem((N * OROW, LIVE), BF16),
            vmem((HOLD, 2 * FP, PW), BF16),
            vmem((NY, FP, DO // NY), BF16),
            vmem((LIVE, 2 * FP), F32),
            vmem((LIVE, FP), BF16),
            vmem((HOLD, LIVE, PW), BF16),
            vmem((2, 8, H1, OW), BF16),
            vmem((2, 8, T1, OW), BF16),
            vmem((8, T1, OW), BF16),
            vmem((2, 4, T1, OW), BF16),
            vmem((2, 4, NY, T2, OW), BF16),
            vmem((2, H2, OW), BF16),
            vmem((2, T2, OW), BF16),
            vmem((LIVE, OW), BF16),
            vmem((N, OROW, OW), BF16),
            vmem((HOLD, OROW, OW), BF16),
            dma((8,)),
            dma,
            dma,
            dma((4, STEPS)),
            dma((4, NSUB, STEPS)),
            dma((2, 8)),
            dma((2, 8)),
            dma((2, 8)),
            dma((2, 8)),
            dma((2, 4)),
            dma((2, 4)),
            dma((2, 4, NY)),
            dma((2, 4, NY)),
            dma((2,)),
            dma((2,)),
            dma((2,)),
            dma((2,)),
            dma,
            dma,
        ],
        compiler_params=pltpu.CompilerParams(
            collective_id=0, has_side_effects=True, vmem_limit_bytes=60 * 2**20
        ),
        cost_estimate=pl.CostEstimate(flops=10**10, bytes_accessed=12 * 10**6, transcendentals=LIVE * FF),
        name="swiglu",
    )(counts, tv, ts, gv, gs, uv, us, dv, ds)


def solution(mesh):
    rows, split = P(("replica", "group"), None), P("group", None)
    in_specs = (rows, rows, P("replica")) + (split,) * 6
    return jax.shard_map(shards, mesh=mesh, in_specs=in_specs, out_specs=rows, check_vma=False)
```

time: 476 us -> 163 us (0.34)
  waiting for transfers between devices: 326 us -> 0 us
  Pallas kernels: 0 us -> 155 us
  matrix products: 59.1 us -> 0 us
  blocking collectives: 52.8 us -> 0 us
  local copies, waits for them, and re-layouts: 23.2 us -> 6.57 us
  between operations: 13.4 us -> 0.01 us
    reduce_scatter x1 -> x0, waiting for transfers between devices: 229 us -> none  [shards(): lax.psum_scatter(rounded(jnp.dot(hidden, w_down, preferred_element_type=j...]
    pallas_call x0 -> x1, Pallas kernels: none -> 155 us  [shards(): pl.pallas_call(kernel, out_shape=jax.ShapeDtypeStruct((CAP, DO), BF16), i...]
    all_gather x1 -> x0, waiting for transfers between devices: 96.5 us -> none  [shards(): lax.all_gather(token_values, 'group', axis=0, tiled=True)]
    dot_general x3 -> x0, matrix products: 59.1 us -> none  [the longest x1 24.3 us: shards(): lax.dot_general(token_rows, w_up, contract, preferred_element_type=jnp.fl...]
    all_gather x1 -> x0, blocking collectives: 52.8 us -> none  [shards(): lax.all_gather(token_scales, 'group', axis=0, tiled=True)]
    mul x4 -> x0, local copies, waits for them, and re-layouts: 19 us -> none  [dequant(): values.astype(jnp.float32).reshape(row_count, blocks, feat_width // blocks)]
  transfers between devices with their start and end apart: 2 -> 0, of which waited for: 2 -> 0; matrix products, arithmetic and copies ran while one was open for 1% -> 0% of each run, Pallas kernels for 0% -> 0%
where the time goes in v1:
time: 163 us; the launch traced here: 162 us
  Pallas kernels  155 us (95%)
  local copies, waits for them, and re-layouts  6.57 us (4%)
    pallas_call x1, Pallas kernels, shards(): pl.pallas_call(kernel, out_shape=jax.ShapeDtypeStruct((CAP, DO), BF16), i...  155 us
    unnamed x4, local copies, waits for them, and re-layouts  6.57 us

profile of v1, /device:TPU:4, one launch (start us, length us, event | category | flops | bytes accessed | tf_op | source)
XLA Modules:
  0.0 161.9 jit_solution(13360679055812743517)
XLA Ops:
  0.0 1.7 %copy.10.gs_h = f32[288,56]{1,0:T(8,128)} copy(f32[288,56]{0,1:T(8,128)} %param.13) | data formatting | bytes 129024 | tf_op args[4]
  1.7 1.7 %copy.11.us_h = f32[288,56]{1,0:T(8,128)} copy(f32[288,56]{0,1:T(8,128)} %param.15) | data formatting | bytes 129024 | tf_op args[6]
  3.3 1.6 copy.12.ds_h
  4.9 155.4 %swiglu.1 = bf16[40,3584]{1,0:T(8,128)(2,1)} custom-call(s32[32]{0:T(128)} %counts.1, bf16[40,7168]{1,0:T(8,128)(2,1)} %tv_h.1, bf16[40,56]{1,0:T(8,128)(2,1)} %ts_h.1, bf16[288,7168]{1,0:T(8,128)(2,1)} %gv_h.1, f32[288,56]{1,0:T(8,128)} %copy.10.gs_h, bf16[288,7168]{1,0:T(8,128)(2,1)} %uv_h.1, f32[288,56]{1,0:T(8,128)} %copy.11.us_h, ...), custom_call_target="tpu_custom_call" | custom-call | flops 10000000000 | bytes 12000000 | tf_op jit(solution)/shard_map/swiglu/pallas_call | solution.py:498
  160.2 1.7 %copy.14 = bf16[40,3584]{1,0:T(8,128)(2,1)} copy(bf16[40,3584]{1,0:T(8,128)(2,1)} %swiglu.1) | data formatting | bytes 573440

commit v2 on v1

--- a/solution.py
+++ b/solution.py
@@ -12,9 +12,6 @@
 HOLD = 28
 PW, OW = 256, 128
 HALF = LIVE // 2
-NSUB = 4
-SUB = HALF // NSUB
-STEPS = N // 2
 FP = 384
 T1 = 480
 T2 = LIVE - T1
@@ -22,19 +19,46 @@
 OROW = 48
 ORDER = (4, 3, -3, 2, -2, 1, -1, 0)
 
+ARRIVALS = (
+    ("z1", 0, 0, 0), ("z1", 1, 0, 1), ("y2", 0, 0), ("y2", 1, 0), ("z1", 0, 0, 1), ("z1", 1, 0, 0),
+    ("y1", 0, 0, 0, 0), ("y1", 1, 0, 0, 1), ("y1", 0, 0, 0, 1), ("y1", 1, 0, 0, 0), ("z2", 0, 0, 0), ("z2", 1, 0, 0),
+    ("y1", 0, -1, 0, 0), ("y1", 1, -1, 0, 0), ("z1", 0, 1, 0), ("z1", 1, 1, 1), ("y1", 0, 1, 0, 1),
+    ("y1", 1, 1, 0, 1), ("z2", 0, 0, 3), ("z2", 1, 0, 3), ("y2", 0, 1), ("y2", 1, 1), ("z2", 0, 0, 1),
+    ("z2", 1, 0, 1), ("y1", 0, -1, 0, 1), ("y1", 1, -1, 0, 1), ("z1", 0, 1, 1), ("z1", 1, 1, 0), ("y1", 0, 1, 0, 0),
+    ("y1", 1, 1, 0, 0), ("y1", 0, 0, 1, 0), ("y1", 1, 0, 1, 1), ("z2", 0, 1, 0), ("z2", 1, 1, 0), ("y1", 0, -1, 1, 0),
+    ("y1", 1, -2, 0, 0), ("z1", 0, 2, 0), ("z1", 1, 2, 1), ("y1", 0, -2, 0, 0), ("y1", 1, 2, 0, 1), ("z2", 0, 1, 3),
+    ("z2", 1, 1, 3), ("y1", 0, 2, 0, 1), ("y1", 1, 1, 1, 1), ("z2", 0, 0, 2), ("z2", 1, 0, 2), ("y1", 0, -2, 0, 1),
+    ("y1", 1, -1, 1, 1), ("z2", 0, 1, 1), ("z2", 1, 1, 1), ("y1", 0, 2, 0, 0), ("y1", 1, -2, 0, 1), ("z1", 0, 2, 1),
+    ("z1", 1, 2, 0), ("y1", 0, 1, 1, 0), ("y1", 1, 2, 0, 0), ("z2", 0, 2, 0), ("z2", 1, 2, 0), ("y1", 0, -3, 0, 0),
+    ("y1", 1, -3, 0, 0), ("z1", 0, 3, 0), ("z1", 1, 3, 1), ("y1", 0, 3, 0, 1), ("y1", 1, 3, 0, 1),
+    ("y1", 0, -2, 1, 0), ("y1", 1, 2, 1, 1), ("z2", 0, 2, 3), ("z2", 1, 2, 3), ("y1", 0, 2, 1, 0),
+    ("y1", 1, -2, 1, 1), ("z2", 0, 1, 2), ("z2", 1, 1, 2), ("y1", 0, -3, 0, 1), ("y1", 1, -3, 0, 1), ("z2", 0, 2, 1),
+    ("z2", 1, 2, 1), ("y1", 0, 3, 0, 0), ("y1", 1, 3, 0, 0), ("z2", 0, 3, 0), ("z2", 1, 3, 0), ("z2", 0, 3, 3),
+    ("z2", 1, 3, 3), ("y1", 0, -3, 1, 0), ("y1", 1, 4, 0, 0), ("z2", 0, 2, 2), ("z2", 1, 2, 2), ("y1", 0, 4, 0, 0),
+    ("y1", 1, 4, 0, 1), ("z2", 0, 3, 1), ("z2", 1, 3, 1), ("y1", 0, 4, 0, 1), ("y1", 1, 3, 1, 1), ("z2", 0, 3, 2),
+    ("z2", 1, 3, 2), ("y1", 0, 3, 1, 0), ("y1", 1, -3, 1, 1), ("y1", 0, 4, 1, 0), ("y1", 1, 4, 1, 1),
+)
+
 
 def kernel(
     counts, tv_h, ts_h, gv_h, gs_h, uv_h, us_h, dv_h, ds_h, out,
-    tv, ts, gv, gs, uv, us, dv, ds, asrc, adst, xs, onehot, back, w, wd, acc, hid, ring,
+    tv, ts, gv, gs, gst, uv, us, ust, dv, ds, dst, asrc, adst, xs, onehot, back, w, wd, acc, hid, ring,
     r1, r2, yz, zr, tz, ty1, ty2, res, osrc, odst,
-    ld, a_s, a_r, g_s, g_r, s1, q1, s2, q2, sz, qz, st, qt, sy1, qy1, sy2, qy2, o_s, o_r,
+    ld, a_s, a_r, z1_s, z1_r, y1_s, y1_r, y2_s, y2_r, z2_s, z2_r, s1, q1, s2, q2, sz, qz, st, qt, sy1, qy1, sy2, qy2, o_s, o_r,
 ):
     rep = lax.axis_index("replica")
     g = lax.axis_index("group")
     z, y = g // NY, g % NY
     up_y, dn_y = z * NY + (y + 1) % NY, z * NY + (y + 3) % NY
     up_z, dn_z = ((z + 1) % NZ) * NY + y, ((z + 7) % NZ) * NY + y
-    is_holder = g < HOLD
+    def holds(dev):
+        return dev % 9 != 0
+
+    def piece_of(dev):
+        return jnp.maximum(dev - 1 - dev // 9, 0)
+
+    is_holder = holds(g)
+    mine = piece_of(g)
 
     def remote(src, dst, send, recv, to):
         return pltpu.make_async_remote_copy(
@@ -44,7 +68,7 @@
     loads = [
         pltpu.make_async_copy(a, b, ld.at[i])
         for i, (a, b) in enumerate(
-            ((tv_h, tv), (ts_h, ts), (gv_h, gv), (gs_h, gs), (uv_h, uv), (us_h, us), (dv_h, dv), (ds_h, ds))
+            ((tv_h, tv), (ts_h, ts), (gv_h, gv), (gs_h, gst), (uv_h, uv), (us_h, ust), (dv_h, dv), (ds_h, dst))
         )
     ]
     for load in loads:
@@ -69,9 +93,9 @@
     def scatter(i, c):
         to = (g + i) % N
 
-        @pl.when(to < HOLD)
+        @pl.when(holds(to))
         def _():
-            remote(asrc.at[to], adst.at[g], a_s, a_r, to).start()
+            remote(asrc.at[piece_of(to)], adst.at[g], a_s, a_r, to).start()
 
         return c
 
@@ -95,9 +119,10 @@
 
     lax.fori_loop(0, LIVE // 16, build, 0)
 
-    for v, s, at in ((gv, gs, 0), (uv, us, FP)):
+    for v, s, st_, at in ((gv, gs, gst, 0), (uv, us, ust, FP)):
         loads[2 if at == 0 else 4].wait()
         loads[3 if at == 0 else 5].wait()
+        s[...] = st_[...].T
 
         def deq(r, c, v=v, s=s, at=at):
             r0 = pl.multiple_of(r * 32, 32)
@@ -109,6 +134,21 @@
 
         lax.fori_loop(0, FF // 32, deq, 0)
 
+    loads[6].wait()
+    loads[7].wait()
+    ds[...] = dst[...].T
+
+    def deq_down(r, c):
+        r0 = pl.multiple_of(r * 32, 32)
+        sf = ds[pl.ds(r0, 32), :]
+        for b in range(HOLD):
+            val = dv[pl.ds(r0, 32), 128 * b : 128 * b + 128].astype(F32) * sf[:, b : b + 1]
+            wd[b % NY, pl.ds(r0, 32), 128 * (b // NY) : 128 * (b // NY) + 128] = val.astype(BF16)
+        return c
+
+    lax.fori_loop(0, FF // 32, deq_down, 0)
+    wd[:, FF:, :] = jnp.zeros((NY, FP - FF, DO // NY), BF16)
+
     def pad(p, c):
         w[p, FF:FP, :] = jnp.zeros((FP - FF, PW), BF16)
         w[p, FP + FF :, :] = jnp.zeros((FP - FF, PW), BF16)
@@ -119,7 +159,7 @@
 
     @pl.when(is_holder)
     def _():
-        adst[g] = asrc[g]
+        adst[g] = asrc[mine]
         pltpu.make_async_copy(adst.at[pl.ds(0, N - 1)], adst.at[pl.ds(0, N - 1)], a_r).wait()
 
         def spread(k, c):
@@ -132,99 +172,154 @@
 
         lax.fori_loop(0, N // 2, spread, 0)
 
-    corner = (y + z) % NY
-    nxt = (
-        jnp.where(corner == 3, up_z, up_y),
-        jnp.where(corner == 0, dn_z, dn_y),
-        jnp.where(corner == 3, up_y, up_z),
-        jnp.where(corner == 0, dn_y, dn_z),
-    )
-    turn = (z + 32 - 3 * y) % NZ
-    pos_a = NY * z + corner
-    pos_b = jnp.where(turn < 4, 4 * y + turn, 4 * (y + 4) + turn - 4)
-
-    def source(q, d):
-        p = ((pos_a if q < 2 else pos_b) + (64 - d if q % 2 == 0 else d)) % N
-        hi, r = p // 4, p % 4
-        if q < 2:
-            return hi * NY + (r + 8 - hi) % NY
-        return ((3 * hi + r) % NZ) * NY + hi % NY
-
-    def last(q, u):
-        return (u < NSUB // 2) == (q % 2 == 0)
-
-    def piece(q, u, src):
-        return ring.at[src, pl.ds((q // 2) * HALF + u * SUB, SUB), :]
-
-    def forward(q, u, src, d):
-        ref = piece(q, u, src)
-        return remote(ref, ref, g_s.at[q, d], g_r.at[q, u, d], nxt[q])
-
     def multiply(src, r0, n):
-        acc[pl.ds(r0, n), :] += lax.dot_general(
-            ring[src, pl.ds(r0, n), :], w[src], (((1,), (1,)), ((), ())), preferred_element_type=F32
+        acc[r0 : r0 + n, :] += lax.dot_general(
+            ring[src, r0 : r0 + n, :], w[src], (((1,), (1,)), ((), ())), preferred_element_type=F32
         )
+
+    def at(dz, dy):
+        dev = ((z + dz + 8) % NZ) * NY + (y + dy + 4) % NY
+        return holds(dev), piece_of(dev)
+
+    def when(dz, dy, f):
+        live, p = at(dz, dy)
+        pl.when(live)(lambda: f(p))
+
+    to_z, to_y = (up_z, dn_z), (up_y, dn_y)
+
+    def over(ref, sem):
+        pltpu.make_async_copy(ref, ref, sem).wait()
+
+    def gathered():
+        for way in range(2):
+            for step in range(4):
+                n1, n2 = (T1, T2) if step < 3 else (H1, H2)
+                when(-sgn(way) * step, 0, lambda p: over(ring.at[0, 0:n1, :], z1_s.at[way, step]))
+                whole = (z + step) % 2 == 1
+                pl.when(whole)(lambda: over(ring.at[0:NY, 0:n2, :], z2_s.at[way, step]))
+                pl.when(jnp.logical_not(whole))(lambda: over(ring.at[0 : NY - 1, 0:n2, :], z2_s.at[way, step]))
+            over(ring.at[0:7, 0 : T1 + H1, :], y1_s.at[way])
+            when(0, 0, lambda p: y2(way, 0, p).wait_send())
+            when(0, -sgn(way), lambda p: y2(way, 1, p).wait_send())
+
+    def sgn(way):
+        return 1 - 2 * way
+
+    def z1(way, step, half, p):
+        ref = ring.at[p, pl.ds(half * H1, H1), :]
+        return remote(ref, ref, z1_s.at[way, step], z1_r.at[way, step, half], to_z[way])
+
+    def y1(way, e, step, half, p):
+        ref = ring.at[p, pl.ds(half * H1, H1), :]
+        i = e % NZ
+        return remote(ref, ref, y1_s.at[way], y1_r.at[way, i, half if step == 0 else 2], to_y[way])
+
+    def y2(way, step, p):
+        ref = ring.at[p, pl.ds(T1, T2), :] if step == 0 else ring.at[p, pl.ds(T1 + way * H2, H2), :]
+        return remote(ref, ref, y2_s.at[way, step], y2_r.at[way, step], to_y[way])
+
+    def z2(way, step, dy, p):
+        ref = ring.at[p, pl.ds(T1, T2), :] if step < 3 else ring.at[p, pl.ds(T1 + way * H2, H2), :]
+        return remote(ref, ref, z2_s.at[way, step], z2_r.at[way, step, dy], to_z[way])
+
+    def y1_send(e, half):
+        def f(p):
+            for way in range(2):
+                y1(way, e, 0, half, p).start()
+
+        when(e, 0, f)
+
+    def z2_send(dy):
+        def f(p):
+            for way in range(2):
+                z2(way, 0, dy, p).start()
+
+        when(0, dy, f)
+
+    def take_z1(way, step, half):
+        d = step + 1
+
+        def f(p):
+            z1(way, step, half, p).wait_recv()
+            if d < 3 or (d == 3 and half == way):
+                z1(way, d, half, p).start()
+
+        when(-sgn(way) * d, 0, f)
+        y1_send(-sgn(way) * d, half)
+
+    def take_y1(way, e, step, half):
+        def f(p):
+            y1(way, e, step, half, p).wait_recv()
+            if step == 0 and half == way:
+                y1(way, e, 1, half, p).start()
+
+        when(e, -sgn(way) * (step + 1), f)
+
+    def take_y2(way, step):
+        def f(p):
+            y2(way, step, p).wait_recv()
+            if step == 0:
+                y2(way, 1, p).start()
+
+        when(0, -sgn(way) * (step + 1), f)
+        if step == 0:
+            z2_send(-sgn(way) % NY)
+        elif way == 1:
+            z2_send(2)
+
+    def take_z2(way, step, dy):
+        d = step + 1
+
+        def f(p):
+            z2(way, step, dy, p).wait_recv()
+            if d < 4:
+                z2(way, d, dy, p).start()
+
+        when(-sgn(way) * d, dy, f)
+
+    takes = {"z1": take_z1, "y1": take_y1, "y2": take_y2, "z2": take_z2}
+
+    def column(e, lo, hi):
+        def body(i, c):
+            when(e, jnp.where(i < 2, i, 5 - i), lambda p: multiply(p, 0, T1))
+            return c
+
+        lax.fori_loop(lo, hi, body, 0)
+
+    def ring_of(d):
+        def body(i, c):
+            dz = d if d in (0, 4) else jnp.where(i < NY, d, -d)
+            when(dz, i % NY, lambda p: multiply(p, T1, T2))
+            return c
+
+        lax.fori_loop(0, NY if d in (0, 4) else 2 * NY, body, 0)
 
     @pl.when(is_holder)
     def _():
         for h in range(2):
-            ring[g, pl.ds(h * HALF, HALF), :] = jnp.dot(
+            ring[mine, pl.ds(h * HALF, HALF), :] = jnp.dot(
                 onehot[pl.ds(h * HALF, HALF), :], xs[...], preferred_element_type=F32
             ).astype(BF16)
-            for u in range(NSUB):
-                for q in (2 * h, 2 * h + 1):
-                    forward(q, u, g, 0).start()
-        multiply(g, 0, HALF)
-        multiply(g, HALF, HALF)
-
-    loads[6].wait()
-    loads[7].wait()
-
-    def deq_down(r, c):
-        r0 = pl.multiple_of(r * 32, 32)
-        sf = ds[pl.ds(r0, 32), :]
-        for b in range(HOLD):
-            val = dv[pl.ds(r0, 32), 128 * b : 128 * b + 128].astype(F32) * sf[:, b : b + 1]
-            wd[b % NY, pl.ds(r0, 32), 128 * (b // NY) : 128 * (b // NY) + 128] = val.astype(BF16)
-        return c
-
-    lax.fori_loop(0, FF // 32, deq_down, 0)
-    wd[:, FF:, :] = jnp.zeros((NY, FP - FF, DO // NY), BF16)
-
-    def gather(t, c):
-        srcs = [source(q, t + 1) for q in range(4)]
-        for u in range(NSUB):
-            for q in range(4):
-
-                @pl.when(srcs[q] < HOLD)
-                def _(q=q, u=u):
-                    forward(q, u, srcs[q], t).wait_recv()
-                    if last(q, u):
-                        forward(q, u, srcs[q], t + 1).start()
-                    else:
-
-                        @pl.when(t < STEPS - 2)
-                        def _():
-                            forward(q, u, srcs[q], t + 1).start()
-
-        for q in range(4):
-
-            @pl.when(srcs[q] < HOLD)
-            def _(q=q):
-                multiply(srcs[q], (q // 2) * HALF, HALF)
-
-        return c
-
-    lax.fori_loop(0, STEPS - 1, gather, 0)
-    for q in range(4):
-        src = source(q, STEPS)
-
-        @pl.when(src < HOLD)
-        def _(q=q, src=src):
-            for u in range(NSUB):
-                if last(q, u):
-                    forward(q, u, src, STEPS - 1).wait_recv()
-            multiply(src, (q // 2) * HALF + (q % 2) * (HALF // 2), HALF // 2)
+        for way in range(2):
+            y2(way, 0, mine).start()
+        for i in range(2):
+            for way in range(2):
+                z1(way, 0, i if way == 0 else 1 - i, mine).start()
+
+    y1_send(0, 0)
+    y1_send(0, 1)
+    z2_send(0)
+    for n, (wave, *which) in enumerate(ARRIVALS):
+        takes[wave](*which)
+        later = ARRIVALS[n + 1 :]
+        if wave == "z2" and not any(o[0] == "z2" and o[2] == which[1] for o in later):
+            ring_of(which[1] + 1)
+        if wave == "y2" and not any(o[0] == "y2" for o in later):
+            ring_of(0)
+        if wave == "y1" and not any(o[0] == "y1" and o[2] == which[1] for o in later):
+            column(which[1], 3 if which[1] == 4 else 0, 4)
+        elif wave == "y1" and which[1:3] == [4, 0] and not any(o[0] == "y1" and o[2:4] == (4, 0) for o in later):
+            column(4, 0, 3)
 
     for r in range(LIVE // 128):
         rows = pl.ds(r * 128, 128)
@@ -252,13 +347,13 @@
 
     def m1(k, up):
         if up:
-            return remote(part(zps[k], 2, 0, H1), r1.at[0, k], s1.at[0, k], q1.at[0, k], up_y)
-        return remote(part(zps[k], 2, H1, H1), r1.at[1, k], s1.at[1, k], q1.at[1, k], dn_y)
+            return remote(part(zps[k], 2, 0, H1), r1.at[0, k], s1.at[0], q1.at[0, k], up_y)
+        return remote(part(zps[k], 2, H1, H1), r1.at[1, k], s1.at[1], q1.at[1, k], dn_y)
 
     def m2(k, up):
         if up:
-            return remote(part(zps[k], 1, 0, T1), r2.at[0, k], s2.at[0, k], q2.at[0, k], up_y)
-        return remote(part(zps[k], 3, 0, T1), r2.at[1, k], s2.at[1, k], q2.at[1, k], dn_y)
+            return remote(part(zps[k], 1, 0, T1), r2.at[0, k], s2.at[0], q2.at[k], up_y)
+        return remote(part(zps[k], 3, 0, T1), r2.at[1, k], s2.at[1], q2.at[k], dn_y)
 
     def mz(k, way, dist):
         to = up_z if way == 0 else dn_z
@@ -273,9 +368,9 @@
         if dist == 4:
             src = w.at[p, pl.ds(T1 + way * H2, H2), 0:OW]
             dst = tz.at[way, 3, yp, pl.ds(way * H2, H2), :]
-            return remote(src, dst, st.at[way, 3, yp], qt.at[way, 3, yp], to)
+            return remote(src, dst, st.at[way, 3], qt.at[way, 3, yp], to)
         src = w.at[p, pl.ds(T1, T2), 0:OW]
-        return remote(src, tz.at[way, dist - 1, yp], st.at[way, dist - 1, yp], qt.at[way, dist - 1, yp], to)
+        return remote(src, tz.at[way, dist - 1, yp], st.at[way, dist - 1], qt.at[way, dist - 1, yp], to)
 
     def my1(up):
         if up:
@@ -304,8 +399,8 @@
         dz = ORDER[k]
 
         def f():
-            m2(k, True).wait_recv()
-            m2(k, False).wait_recv()
+            both = r2.at[:, k]
+            pltpu.make_async_copy(both, both, q2.at[k]).wait()
             ways = {4: (), 0: (0, 1)}.get(dz, (0,) if dz > 0 else (1,))
             for way in ways:
                 mz(k, way, abs(dz) + 1).wait_recv()
@@ -414,6 +509,7 @@
         hit = (diff == offs[i]) & (jrow < counts[i])
         back[i * OROW : (i + 1) * OROW, :] = jnp.where(hit, 1.0, 0.0).astype(BF16)
 
+    gathered()
     line(5)
     line(6)
     line(7)
@@ -437,42 +533,30 @@
 
         lax.fori_loop(1, N, give, 0)
 
-    def drain(t, c):
-        for q in range(4):
-
-            @pl.when(source(q, t) < HOLD)
-            def _(q=q):
-                ref = ring.at[0, pl.ds(0, HALF), :]
-                pltpu.make_async_copy(ref, ref, g_s.at[q, t]).wait()
-
-        return c
-
-    lax.fori_loop(0, STEPS - 1, drain, 0)
-    for q in range(4):
-
-        @pl.when(source(q, STEPS - 1) < HOLD)
-        def _(q=q):
-            ref = ring.at[0, pl.ds(0, HALF // 2), :]
-            pltpu.make_async_copy(ref, ref, g_s.at[q, STEPS - 1]).wait()
-
-    for k in range(8):
-
-        def f(k=k):
-            dz = ORDER[k]
-            for way in range(2):
-                m1(k, way == 0).wait_send()
-                m2(k, way == 0).wait_send()
-                if dz == 4 or (dz > 0 and way == 0) or (dz < 0 and way == 1):
-                    mz(k, way, abs(dz)).wait_send()
-                    for yp in range(NY):
-                        mt(k, way, abs(dz), yp).wait_send()
-
-        guarded(k, f)
+    for way in range(2):
+        over(r1.at[way, 0:7], s1.at[way])
+        over(r2.at[way, 0:7], s2.at[way])
+        for k, dz in enumerate(ORDER):
+            if dz == 4 or (dz > 0 and way == 0) or (dz < 0 and way == 1):
+
+                def f(k=k, way=way, dist=abs(dz)):
+                    mz(k, way, dist).wait_send()
+                    over(tz.at[way, 0, :, 0 : H2 if dist == 4 else T2, :], st.at[way, dist - 1])
+
+                guarded(k, f)
 
     @pl.when(is_holder)
     def _():
         some = asrc.at[pl.ds(0, HOLD - 1)]
         pltpu.make_async_copy(some, some, a_s).wait()
+
+    @pl.when(jnp.logical_not(is_holder))
+    def _():
+        some = asrc.at[pl.ds(0, HOLD)]
+        pltpu.make_async_copy(some, some, a_s).wait()
+
+    @pl.when(z < 7)
+    def _():
         for way in range(2):
             my1(way == 0).wait_send()
             my2(way == 0).wait_send()
@@ -481,10 +565,8 @@
         some = osrc.at[pl.ds(0, N - 1)]
         pltpu.make_async_copy(some, some, o_s).wait()
 
-    @pl.when(g >= HOLD)
+    @pl.when(z == 7)
     def _():
-        some = asrc.at[pl.ds(0, HOLD)]
-        pltpu.make_async_copy(some, some, a_s).wait()
         some = odst.at[pl.ds(0, HOLD)]
         pltpu.make_async_copy(some, some, o_r).wait()
 
@@ -505,10 +587,13 @@
             vmem((CAP, D // 128), BF16),
             vmem((FF, D), BF16),
             vmem((FF, D // 128), F32),
+            vmem((D // 128, FF), F32),
             vmem((FF, D), BF16),
             vmem((FF, D // 128), F32),
+            vmem((D // 128, FF), F32),
             vmem((FF, DO), BF16),
             vmem((FF, DO // 128), F32),
+            vmem((DO // 128, FF), F32),
             vmem((HOLD, 2 * CAP, 128), BF16),
             vmem((N, 2 * CAP, 128), BF16),
             vmem((N * CAP, PW), BF16),
@@ -532,15 +617,21 @@
             dma((8,)),
             dma,
             dma,
-            dma((4, STEPS)),
-            dma((4, NSUB, STEPS)),
+            dma((2, 4)),
+            dma((2, 4, 2)),
+            dma((2,)),
+            dma((2, NZ, 3)),
+            dma((2, 2)),
+            dma((2, 2)),
+            dma((2, 4)),
+            dma((2, 4, NY)),
+            dma((2,)),
             dma((2, 8)),
-            dma((2, 8)),
-            dma((2, 8)),
-            dma((2, 8)),
+            dma((2,)),
+            dma((8,)),
             dma((2, 4)),
             dma((2, 4)),
-            dma((2, 4, NY)),
+            dma((2, 4)),
             dma((2, 4, NY)),
             dma((2,)),
             dma((2,)),
@@ -554,7 +645,7 @@
         ),
         cost_estimate=pl.CostEstimate(flops=10**10, bytes_accessed=12 * 10**6, transcendentals=LIVE * FF),
         name="swiglu",
-    )(counts, tv, ts, gv, gs, uv, us, dv, ds)
+    )(counts, tv, ts, gv, gs.T, uv, us.T, dv, ds.T)
 
 
 def solution(mesh):

time: 163 us -> 151 us (0.926)
  Pallas kernels: 155 us -> 148 us
  local copies, waits for them, and re-layouts: 6.57 us -> 1.69 us
    pallas_call x1, Pallas kernels: 155 us -> 148 us  [shards(): pl.pallas_call(kernel, out_shape=jax.ShapeDtypeStruct((CAP, DO), BF16), i...]
    unnamed x4 -> x1, local copies, waits for them, and re-layouts: 6.57 us -> 1.69 us
where the time goes in v2:
time: 151 us; the launch traced here: 150 us
  Pallas kernels  148 us (98%)
  local copies, waits for them, and re-layouts  1.69 us (1%)
    pallas_call x1, Pallas kernels, shards(): pl.pallas_call(kernel, out_shape=jax.ShapeDtypeStruct((CAP, DO), BF16), i...  148 us

profile of v2, /device:TPU:4, one launch (start us, length us, event | category | flops | bytes accessed | tf_op | source)
XLA Modules:
  0.0 150.1 jit_solution(5678555429312411723)
XLA Ops:
  0.0 148.4 %swiglu.1 = bf16[40,3584]{1,0:T(8,128)(2,1)} custom-call(s32[32]{0:T(128)} %counts.1, bf16[40,7168]{1,0:T(8,128)(2,1)} %tv_h.1, bf16[40,56]{1,0:T(8,128)(2,1)} %ts_h.1, bf16[288,7168]{1,0:T(8,128)(2,1)} %gv_h.1, f32[56,288]{1,0:T(8,128)} %bitcast.3, bf16[288,7168]{1,0:T(8,128)(2,1)} %uv_h.1, f32[56,288]{1,0:T(8,128)} %bitcast.4, bf16[288,3584]{1,0:T(8,128)(2,1)} %dv_h.1, ...), custom_call_target="tpu_custom_call" | custom-call | flops 10000000000 | bytes 12000000 | tf_op jit(solution)/shard_map/swiglu/pallas_call | solution.py:580
  148.4 1.7 %copy.11 = bf16[40,3584]{1,0:T(8,128)(2,1)} copy(bf16[40,3584]{1,0:T(8,128)(2,1)} %swiglu.1) | data formatting | bytes 573440

commit v3 on v2

v3 whole, which is shorter than its diff:
```python
import jax
import jax.numpy as jnp
from jax import lax
from jax.experimental import pallas as pl
from jax.experimental.pallas import tpu as pltpu
from jax.sharding import PartitionSpec as P

F32, BF16, I32 = jnp.float32, jnp.bfloat16, jnp.int32
N, NZ, NY = 32, 8, 4
CAP, LIVE = 40, 768
D, DO, FF = 7168, 3584, 288
HOLD = 28
PW, OW = 256, 128
HALF = LIVE // 2
FP = 384
T1 = 448
T2 = LIVE - T1
H1, H2 = T1 // 2, T2 // 2
S1 = 448
S2 = LIVE - S1
K1, K2 = S1 // 2, S2 // 2
HELD = tuple(d for d in range(N) if d % 9)
OROW = 48
ORDER = (4, 3, -3, 2, -2, 1, -1, 0)

ARRIVALS = (
    ("z1", 1, 0, 1), ("z1", 0, 0, 0), ("y2", 1, 0), ("z1", 0, 0, 1), ("y2", 0, 0), ("z1", 0, 1, 0), ("z1", 1, 1, 1),
    ("y1", 0, -1, 0, 0), ("y1", 1, 0, 0, 0), ("y1", 0, 0, 0, 1), ("z1", 1, 0, 0), ("y1", 1, -1, 0, 1),
    ("y1", 1, -1, 0, 0), ("y2", 0, 1), ("y2", 1, 1), ("z1", 0, 1, 1), ("z1", 1, 2, 1), ("y1", 1, 2, 0, 1),
    ("z2", 0, 0, 1), ("y1", 1, 1, 0, 1), ("z2", 1, 0, 0), ("z1", 1, 1, 0), ("y1", 0, 1, 0, 1), ("z2", 0, 0, 3),
    ("y1", 0, 0, 0, 0), ("z2", 1, 0, 3), ("z1", 1, 3, 1), ("z2", 0, 0, 0), ("z2", 1, 0, 2), ("y1", 0, -2, 0, 1),
    ("y1", 1, 0, 0, 1), ("z2", 0, 0, 2), ("z1", 0, 2, 1), ("y1", 0, -1, 1, 0), ("z1", 0, 2, 0), ("y1", 0, 1, 0, 0),
    ("z2", 1, 0, 1), ("z1", 1, 2, 0), ("z2", 0, 1, 1), ("z2", 1, 1, 0), ("z2", 1, 1, 2), ("z2", 0, 1, 0),
    ("y1", 0, 2, 0, 0), ("y1", 0, 4, 0, 1), ("z2", 0, 1, 3), ("y1", 1, -2, 0, 1), ("y1", 1, 2, 0, 0),
    ("y1", 0, -2, 0, 0), ("y1", 0, -1, 0, 1), ("z2", 1, 1, 1), ("y1", 0, 3, 0, 1), ("y1", 1, -1, 1, 1),
    ("y1", 1, 2, 1, 1), ("z2", 1, 1, 3), ("z2", 0, 1, 2), ("z1", 0, 3, 0), ("y1", 1, -3, 0, 1), ("z2", 0, 2, 1),
    ("y1", 1, -2, 0, 0), ("y1", 1, 0, 1, 1), ("y1", 0, 3, 0, 0), ("y1", 0, 0, 1, 0), ("y1", 0, 2, 1, 0),
    ("y1", 1, 3, 0, 0), ("y1", 1, 3, 0, 1), ("y1", 1, 4, 0, 1), ("y1", 1, -2, 1, 1), ("z2", 1, 2, 0),
    ("y1", 0, 2, 0, 1), ("y1", 1, -3, 0, 0), ("z2", 0, 2, 0), ("y1", 0, -3, 0, 0), ("y1", 0, -2, 1, 0),
    ("z2", 1, 2, 1), ("y1", 1, 1, 0, 0), ("y1", 0, 1, 1, 0), ("y1", 0, 4, 0, 0), ("z2", 0, 2, 3), ("z2", 1, 2, 2),
    ("y1", 1, 1, 1, 1), ("y1", 0, 3, 1, 0), ("z2", 0, 2, 2), ("z2", 1, 2, 3), ("z2", 0, 3, 1), ("y1", 1, 3, 1, 1),
    ("y1", 1, 4, 0, 0), ("z2", 0, 3, 0), ("y1", 0, -3, 0, 1), ("z2", 1, 3, 0), ("y1", 1, 4, 1, 1),
    ("y1", 0, -3, 1, 0), ("z2", 1, 3, 1), ("y1", 1, -3, 1, 1), ("y1", 0, 4, 1, 0), ("z2", 0, 3, 3), ("z2", 0, 3, 2),
    ("z2", 1, 3, 2), ("z2", 1, 3, 3),
)

SUMS = (
    ("tz", 0, 3, 1), ("tz", 1, 3, 0), ("ya", 1, 4), ("tz", 0, 3, 0), ("tz", 0, 3, 3), ("tz", 1, 3, 1),
    ("tz", 1, 3, 2), ("tz", 0, 3, 2), ("ya", 1, -3), ("ya", 0, 4), ("ya", 1, 3), ("tz", 0, 2, 1), ("ya", 0, -3),
    ("tz", 1, 3, 3), ("tz", 0, 2, 0), ("ya", 0, 3), ("ya", 0, -2), ("tz", 1, 2, 0), ("tz", 0, 2, 3), ("ya", 1, -2),
    ("tz", 1, 2, 2), ("ya", 0, 2), ("line", 4), ("tz", 0, 2, 2), ("tz", 1, 2, 1), ("ya", 1, 2), ("ya", 0, 1),
    ("tz", 0, 1, 0), ("ya", 1, -1), ("tz", 1, 2, 3), ("line", -3), ("line", 3), ("tz", 1, 1, 2), ("tz", 0, 1, 2),
    ("ya", 0, 0), ("ya", 1, 0), ("ya", 0, -1), ("tz", 0, 1, 3), ("tz", 1, 1, 3), ("ya", 1, 1), ("line", -2),
    ("line", 2), ("tz", 1, 1, 1), ("tz", 0, 1, 1), ("tz0", 3), ("tz", 1, 1, 0), ("tz0", 2), ("line", -1), ("line", 1),
    ("tz0", 1), ("tz0", 0), ("line", 0), ("fin",),
)


def kernel(
    counts, tv_h, ts_h, gv_h, gs_h, uv_h, us_h, dv_h, ds_h, out,
    tv, ts, gv, gs, gst, uv, us, ust, dv, ds, dst, asrc, adst, xs, onehot, back, w, wd, acc, hid, ring,
    r1, r2, yz, zr, tz, ty, far, res, osrc, odst,
    ld, a_s, a_r, z1_s, z1_r, y1_s, y1_r, y2_s, y2_r, z2_s, z2_r, s1, q1, s2, q2, sz, qz, st, qt, sy, qy, o_s, o_r,
):
    rep = lax.axis_index("replica")
    g = lax.axis_index("group")
    z, y = g // NY, g % NY
    up_y, dn_y = z * NY + (y + 1) % NY, z * NY + (y + 3) % NY
    up_z, dn_z = ((z + 1) % NZ) * NY + y, ((z + 7) % NZ) * NY + y
    def holds(dev):
        return dev % 9 != 0

    def piece_of(dev):
        return jnp.maximum(dev - 1 - dev // 9, 0)

    is_holder = holds(g)
    mine = piece_of(g)

    def remote(src, dst, send, recv, to):
        return pltpu.make_async_remote_copy(
            src, dst, send, recv, device_id=(rep, to), device_id_type=pl.DeviceIdType.MESH
        )

    loads = [
        pltpu.make_async_copy(a, b, ld.at[i])
        for i, (a, b) in enumerate(
            ((tv_h, tv), (ts_h, ts), (gv_h, gv), (gs_h, gst), (uv_h, uv), (us_h, ust), (dv_h, dv), (ds_h, dst))
        )
    ]
    for load in loads:
        load.start()
    barrier = pltpu.get_barrier_semaphore()

    def greet(i, c):
        pl.semaphore_signal(barrier, inc=1, device_id=(rep, (g + i) % N), device_id_type=pl.DeviceIdType.MESH)
        return c

    lax.fori_loop(1, N, greet, 0)

    loads[0].wait()
    loads[1].wait()
    tsf = ts[...].astype(F32)
    for p in range(HOLD):
        lo = tv[:, PW * p : PW * p + 128].astype(F32) * tsf[:, 2 * p : 2 * p + 1]
        hi = tv[:, PW * p + 128 : PW * p + 256].astype(F32) * tsf[:, 2 * p + 1 : 2 * p + 2]
        asrc[p] = jnp.concatenate([lo, hi], axis=0).astype(BF16)
    pl.semaphore_wait(barrier, N - 1)

    def far_first(i):
        k = i // NY
        dz = 4 + (k + 1) // 2 * (1 - 2 * (k % 2))
        return ((z + dz) % NZ) * NY + (y + i) % NY

    def scatter(i, c):
        to = far_first(i)

        @pl.when(holds(to) & (to != g))
        def _():
            remote(asrc.at[piece_of(to)], adst.at[g], a_s, a_r, to).start()

        return c

    lax.fori_loop(0, N, scatter, 0)

    offs, off = [], jnp.int32(0)
    lane = lax.broadcasted_iota(I32, (16, N * CAP), 1)
    target = jnp.full((16, N * CAP), -1, I32)
    for i in range(N):
        c = counts[i]
        rel = lane - CAP * i
        target = jnp.where((rel >= 0) & (rel < c), rel + off, target)
        offs.append(off)
        off = off + c
    row16 = lax.broadcasted_iota(I32, (16, N * CAP), 0)

    def build(r, c):
        hit = target == row16 + r * 16
        onehot[pl.ds(pl.multiple_of(r * 16, 16), 16), :] = jnp.where(hit, 1.0, 0.0).astype(BF16)
        return c

    lax.fori_loop(0, LIVE // 16, build, 0)

    for v, s, st_, at in ((gv, gs, gst, 0), (uv, us, ust, FP)):
        loads[2 if at == 0 else 4].wait()
        loads[3 if at == 0 else 5].wait()
        s[...] = st_[...].T

        def deq(r, c, v=v, s=s, at=at):
            r0 = pl.multiple_of(r * 32, 32)
            sf = s[pl.ds(r0, 32), :]
            for b in range(D // 128):
                val = v[pl.ds(r0, 32), 128 * b : 128 * b + 128].astype(F32) * sf[:, b : b + 1]
                w[b // 2, pl.ds(at + r0, 32), 128 * (b % 2) : 128 * (b % 2) + 128] = val.astype(BF16)
            return c

        lax.fori_loop(0, FF // 32, deq, 0)

    loads[6].wait()
    loads[7].wait()
    ds[...] = dst[...].T

    def deq_down(r, c):
        r0 = pl.multiple_of(r * 32, 32)
        sf = ds[pl.ds(r0, 32), :]
        for b in range(HOLD):
            val = dv[pl.ds(r0, 32), 128 * b : 128 * b + 128].astype(F32) * sf[:, b : b + 1]
            zz, yy = HELD[b] // NY, HELD[b] % NY
            i = zz - int(zz > 2 * yy)
            wd[yy, pl.ds(r0, 32), 128 * i : 128 * i + 128] = val.astype(BF16)
        return c

    lax.fori_loop(0, FF // 32, deq_down, 0)
    wd[:, FF:, :] = jnp.zeros((NY, FP - FF, DO // NY), BF16)

    def pad(p, c):
        w[p, FF:FP, :] = jnp.zeros((FP - FF, PW), BF16)
        w[p, FP + FF :, :] = jnp.zeros((FP - FF, PW), BF16)
        return c

    lax.fori_loop(0, HOLD, pad, 0)
    acc[...] = jnp.zeros_like(acc)

    jrow = lax.broadcasted_iota(I32, (OROW, LIVE), 0)
    diff = lax.broadcasted_iota(I32, (OROW, LIVE), 1) - jrow
    for i in range(N):
        hit = (diff == offs[i]) & (jrow < counts[i])
        back[i * OROW : (i + 1) * OROW, :] = jnp.where(hit, 1.0, 0.0).astype(BF16)

    @pl.when(is_holder)
    def _():
        adst[g] = asrc[mine]
        pltpu.make_async_copy(adst.at[pl.ds(0, N - 1)], adst.at[pl.ds(0, N - 1)], a_r).wait()

        def spread(k, c):
            a = adst[2 * k].astype(F32)
            b = adst[2 * k + 1].astype(F32)
            rows = pl.ds(pl.multiple_of(k * 80, 16), 80)
            xs[rows, 0:128] = jnp.concatenate([a[:CAP], b[:CAP]], axis=0).astype(BF16)
            xs[rows, 128:256] = jnp.concatenate([a[CAP:], b[CAP:]], axis=0).astype(BF16)
            return c

        lax.fori_loop(0, N // 2, spread, 0)

    def multiply(src, r0, n):
        acc[r0 : r0 + n, :] += lax.dot_general(
            ring[src, r0 : r0 + n, :], w[src], (((1,), (1,)), ((), ())), preferred_element_type=F32
        )

    def at(dz, dy):
        dev = ((z + dz + 8) % NZ) * NY + (y + dy + 4) % NY
        return holds(dev), piece_of(dev)

    def when(dz, dy, f):
        live, p = at(dz, dy)
        pl.when(live)(lambda: f(p))

    to_z, to_y = (up_z, dn_z), (up_y, dn_y)

    def over(ref, sem):
        pltpu.make_async_copy(ref, ref, sem).wait()

    def gathered():
        for way in range(2):
            for step in range(4):
                n1, n2 = (T1, T2) if step < 3 else (H1, H2)
                when(-sgn(way) * step, 0, lambda p: over(ring.at[0, 0:n1, :], z1_s.at[way, step]))
                whole = (z + step) % 2 == 1
                pl.when(whole)(lambda: over(ring.at[0:NY, 0:n2, :], z2_s.at[way, step]))
                pl.when(jnp.logical_not(whole))(lambda: over(ring.at[0 : NY - 1, 0:n2, :], z2_s.at[way, step]))
            over(ring.at[0:7, 0 : T1 + H1, :], y1_s.at[way])
            when(0, 0, lambda p: y2(way, 0, p).wait_send())
            when(0, -sgn(way), lambda p: y2(way, 1, p).wait_send())

    def sgn(way):
        return 1 - 2 * way

    def z1(way, step, half, p):
        ref = ring.at[p, pl.ds(half * H1, H1), :]
        return remote(ref, ref, z1_s.at[way, step], z1_r.at[way, step, half], to_z[way])

    def y1(way, e, step, half, p):
        ref = ring.at[p, pl.ds(half * H1, H1), :]
        i = e % NZ
        return remote(ref, ref, y1_s.at[way], y1_r.at[way, i, half if step == 0 else 2], to_y[way])

    def y2(way, step, p):
        ref = ring.at[p, pl.ds(T1, T2), :] if step == 0 else ring.at[p, pl.ds(T1 + way * H2, H2), :]
        return remote(ref, ref, y2_s.at[way, step], y2_r.at[way, step], to_y[way])

    def z2(way, step, dy, p):
        ref = ring.at[p, pl.ds(T1, T2), :] if step < 3 else ring.at[p, pl.ds(T1 + way * H2, H2), :]
        return remote(ref, ref, z2_s.at[way, step], z2_r.at[way, step, dy], to_z[way])

    def y1_send(e, half):
        def f(p):
            for way in range(2):
                y1(way, e, 0, half, p).start()

        when(e, 0, f)

    def z2_send(dy):
        def f(p):
            for way in range(2):
                z2(way, 0, dy, p).start()

        when(0, dy, f)

    def take_z1(way, step, half):
        d = step + 1

        def f(p):
            z1(way, step, half, p).wait_recv()
            if d < 3 or (d == 3 and half == way):
                z1(way, d, half, p).start()

        when(-sgn(way) * d, 0, f)
        y1_send(-sgn(way) * d, half)

    def take_y1(way, e, step, half):
        def f(p):
            y1(way, e, step, half, p).wait_recv()
            if step == 0 and half == way:
                y1(way, e, 1, half, p).start()

        when(e, -sgn(way) * (step + 1), f)

    def take_y2(way, step):
        def f(p):
            y2(way, step, p).wait_recv()
            if step == 0:
                y2(way, 1, p).start()

        when(0, -sgn(way) * (step + 1), f)
        if step == 0:
            z2_send(-sgn(way) % NY)
        elif way == 1:
            z2_send(2)

    def take_z2(way, step, dy):
        d = step + 1

        def f(p):
            z2(way, step, dy, p).wait_recv()
            if d < 4:
                z2(way, d, dy, p).start()

        when(-sgn(way) * d, dy, f)

    takes = {"z1": take_z1, "y1": take_y1, "y2": take_y2, "z2": take_z2}

    def column(e, lo, hi):
        def body(i, c):
            when(e, jnp.where(i < 2, i, 5 - i), lambda p: multiply(p, 0, T1))
            return c

        lax.fori_loop(lo, hi, body, 0)

    def ring_of(d):
        def body(i, c):
            dz = d if d in (0, 4) else jnp.where(i < NY, d, -d)
            when(dz, i % NY, lambda p: multiply(p, T1, T2))
            return c

        lax.fori_loop(0, NY if d in (0, 4) else 2 * NY, body, 0)

    @pl.when(is_holder)
    def _():
        for h in range(2):
            ring[mine, pl.ds(h * HALF, HALF), :] = jnp.dot(
                onehot[pl.ds(h * HALF, HALF), :], xs[...], preferred_element_type=F32
            ).astype(BF16)
        for way in range(2):
            y2(way, 0, mine).start()
        for i in range(2):
            for way in range(2):
                z1(way, 0, i if way == 0 else 1 - i, mine).start()

    y1_send(0, 0)
    y1_send(0, 1)
    z2_send(0)
    for n, (wave, *which) in enumerate(ARRIVALS):
        takes[wave](*which)
        later = ARRIVALS[n + 1 :]
        if wave == "z2" and not any(o[0] == "z2" and o[2] == which[1] for o in later):
            ring_of(which[1] + 1)
        if wave == "y2" and not any(o[0] == "y2" for o in later):
            ring_of(0)
        if wave == "y1" and not any(o[0] == "y1" and o[2] == which[1] for o in later):
            column(which[1], 3 if which[1] == 4 else 0, 4)
        if wave == "y1" and which[1:3] == [4, 0] and not any(o[0] == "y1" and o[2:4] == (4, 0) for o in later):
            column(4, 0, 3)

    for r in range(LIVE // 128):
        rows = pl.ds(r * 128, 128)
        gate = acc[rows, 0:FP]
        hid[rows, :] = (gate / (1.0 + jnp.exp(-gate)) * acc[rows, FP : 2 * FP]).astype(BF16)

    def slab(dy):
        yy = (y + dy) % NY
        for r in range(4):
            rows = pl.ds(r * 192, 192)
            got = jnp.dot(hid[rows, :], wd[yy], preferred_element_type=F32).astype(BF16)
            for i in range(7):
                zz = i + (i >= 2 * yy).astype(I32)
                w[piece_of(zz * NY + yy), rows, 0:OW] = got[:, i * OW : (i + 1) * OW]

    def slab_far(dy):
        yy, zz = (y + dy) % NY, (z + 4) % NZ
        i = zz - (zz > 2 * yy).astype(I32)
        cols = wd[yy, :, pl.ds(pl.multiple_of(i * OW, OW), OW)]
        far[dy] = jnp.dot(hid[S1:, :], cols, preferred_element_type=F32).astype(BF16)

    def part(p, r0, n):
        return w.at[p, r0 : r0 + n, 0:OW]

    def m1(way, e, p):
        return remote(part(p, way * K1, K1), r1.at[way, e % NZ], s1.at[way], q1.at[way, e % NZ], to_y[way])

    def m2(way, e, p):
        return remote(part(p, 0, S1), r2.at[way, e % NZ], s2.at[way], q2.at[e % NZ], to_y[way])

    def mz(way, dist):
        e = sgn(way) * dist % NZ
        if dist == 4:
            rows = pl.ds(way * K1, K1)
            return remote(yz.at[e, rows, :], zr.at[way, 3, rows, :], sz.at[way, 3], qz.at[way, 3], to_z[way])
        return remote(yz.at[e], zr.at[way, dist - 1], sz.at[way, dist - 1], qz.at[way, dist - 1], to_z[way])

    def mt(way, dist, dy, p):
        if dist == 4:
            rows = pl.ds(way * K2, K2)
            src, dst = far.at[dy, rows, :], tz.at[way, 3, dy, rows, :]
        else:
            src, dst = part(p, S1, S2), tz.at[way, dist - 1, dy]
        return remote(src, dst, st.at[way, dist - 1], qt.at[way, dist - 1, dy], to_z[way])

    def my(dy, p):
        to = z * NY + (y + dy) % NY
        return remote(part(p, S1, S2), ty.at[dy - 1], sy.at[dy - 1], qy.at[dy - 1], to)

    def add(ref, *others):
        total = ref[...].astype(F32)
        for other in others:
            total = total + other.astype(F32)
        return total

    def sum_ya(way, e):
        def f(p):
            m1(way, e, p).wait_recv()
            ref = part(p, way * K1, K1)
            ref[...] = add(ref, r1[way, e % NZ]).astype(BF16)
            m2(way, e, p).start()

        when(e, sgn(way), f)

    def sum_line(e):
        ways = {4: (), 0: (0, 1)}.get(e, (0,) if e > 0 else (1,))

        def f(p):
            over(r2.at[:, e % NZ], q2.at[e % NZ])
            for way in ways:
                mz(way, abs(e) + 1).wait_recv()
            for h in range(2):
                rows = pl.ds(h * K1, K1)
                more = [zr[way, abs(e), rows, :] for way in ways if abs(e) < 3 or way == h]
                total = add(part(p, h * K1, K1), r2[0, e % NZ, rows, :], r2[1, e % NZ, rows, :], *more)
                if e == 0:
                    res[rows, :] = total.astype(BF16)
                else:
                    yz[e % NZ, rows, :] = total.astype(BF16)
            if e == 4:
                mz(0, 4).start()
                mz(1, 4).start()
            elif e != 0:
                mz(ways[0], abs(e)).start()

        when(e, 0, f)

    def sum_tz(way, d, dy):
        def f(p):
            mt(way, d + 1, dy, p).wait_recv()
            if d == 3:
                ref, got = part(p, S1 + way * K2, K2), tz[way, 3, dy, pl.ds(way * K2, K2), :]
            else:
                ref, got = part(p, S1, S2), tz[way, d, dy]
            ref[...] = add(ref, got).astype(BF16)
            mt(way, d, dy, p).start()

        when(sgn(way) * d, dy, f)

    def sum_tz0(dy):
        def f(p):
            for way in range(2):
                mt(way, 1, dy, p).wait_recv()
            ref = part(p, S1, S2)
            ref[...] = add(ref, tz[0, 0, dy], tz[1, 0, dy]).astype(BF16)
            if dy:
                my(dy, p).start()

        when(0, dy, f)

    def sum_fin():
        def f(p):
            for dy in range(1, NY):
                my(dy, p).wait_recv()
            res[S1:, :] = add(part(p, S1, S2), ty[0], ty[1], ty[2]).astype(BF16)

        when(0, 0, f)

    sums = {"ya": sum_ya, "line": sum_line, "tz": sum_tz, "tz0": sum_tz0, "fin": sum_fin}
    for dy in range(NY):
        slab_far(dy)
    for dy in range(NY):

        def f(p, dy=dy):
            mt(0, 4, dy, p).start()
            mt(1, 4, dy, p).start()

        when(4, dy, f)
    slab(2)
    for e in ORDER:

        def f(p, e=e):
            m1(0, e, p).start()
            m1(1, e, p).start()

        when(e, 2, f)
    slab(1)
    slab(3)
    slab(0)
    for n, (wave, *which) in enumerate(SUMS):
        if n == len(SUMS) // 2:
            gathered()
        sums[wave](*which)

    @pl.when(is_holder)
    def _():
        for h in range(4):
            slots = jnp.dot(back[h * 384 : (h + 1) * 384, :], res[...], preferred_element_type=F32).astype(BF16)
            for i in range(8):
                osrc[8 * h + i] = slots[i * OROW : (i + 1) * OROW]
        odst[mine] = osrc[g]

        def give(i, c):
            to = far_first(i)

            @pl.when(to != g)
            def _():
                remote(osrc.at[to], odst.at[mine], o_s, o_r, to).start()

            return c

        lax.fori_loop(0, N, give, 0)

    for way in range(2):
        over(r1.at[way, 0:7], s1.at[way])
        over(r2.at[way, 0:7], s2.at[way])
        for dist in range(1, 5):
            when(sgn(way) * dist, 0, lambda p: mz(way, dist).wait_send())
            n2 = S2 if dist < 4 else K2
            whole = (z + dist) % 2 == 1
            pl.when(whole)(lambda: over(tz.at[way, 0, :, 0:n2, :], st.at[way, dist - 1]))
            pl.when(jnp.logical_not(whole))(lambda: over(tz.at[way, 0, 0 : NY - 1, 0:n2, :], st.at[way, dist - 1]))

    for dy in range(1, NY):
        when(0, dy, lambda p: my(dy, p).wait_send())

    @pl.when(is_holder)
    def _():
        over(asrc.at[0 : HOLD - 1], a_s)
        over(odst.at[0 : HOLD - 1], o_r)
        over(osrc.at[0 : N - 1], o_s)

    @pl.when(jnp.logical_not(is_holder))
    def _():
        over(asrc.at[0:HOLD], a_s)
        over(odst.at[0:HOLD], o_r)

    for p in range(HOLD):
        out[:, p * OW : (p + 1) * OW] = odst[p][:CAP]


def shards(tv, ts, counts, gv, gs, uv, us, dv, ds):
    any_space = pl.BlockSpec(memory_space=pl.ANY)
    vmem, dma = pltpu.VMEM, pltpu.SemaphoreType.DMA
    return pl.pallas_call(
        kernel,
        out_shape=jax.ShapeDtypeStruct((CAP, DO), BF16),
        in_specs=[pl.BlockSpec(memory_space=pltpu.SMEM)] + [any_space] * 8,
        out_specs=pl.BlockSpec(memory_space=pltpu.VMEM),
        scratch_shapes=[
            vmem((CAP, D), BF16),
            vmem((CAP, D // 128), BF16),
            vmem((FF, D), BF16),
            vmem((FF, D // 128), F32),
            vmem((D // 128, FF), F32),
            vmem((FF, D), BF16),
            vmem((FF, D // 128), F32),
            vmem((D // 128, FF), F32),
            vmem((FF, DO), BF16),
            vmem((FF, DO // 128), F32),
            vmem((DO // 128, FF), F32),
            vmem((HOLD, 2 * CAP, 128), BF16),
            vmem((N, 2 * CAP, 128), BF16),
            vmem((N * CAP, PW), BF16),
            vmem((LIVE, N * CAP), BF16),
            vmem((N * OROW, LIVE), BF16),
            vmem((HOLD, 2 * FP, PW), BF16),
            vmem((NY, FP, DO // NY), BF16),
            vmem((LIVE, 2 * FP), F32),
            vmem((LIVE, FP), BF16),
            vmem((HOLD, LIVE, PW), BF16),
            vmem((2, 8, K1, OW), BF16),
            vmem((2, 8, S1, OW), BF16),
            vmem((8, S1, OW), BF16),
            vmem((2, 4, S1, OW), BF16),
            vmem((2, 4, NY, S2, OW), BF16),
            vmem((3, S2, OW), BF16),
            vmem((NY, S2, OW), BF16),
            vmem((LIVE, OW), BF16),
            vmem((N, OROW, OW), BF16),
            vmem((HOLD, OROW, OW), BF16),
            dma((8,)),
            dma,
            dma,
            dma((2, 4)),
            dma((2, 4, 2)),
            dma((2,)),
            dma((2, NZ, 3)),
            dma((2, 2)),
            dma((2, 2)),
            dma((2, 4)),
            dma((2, 4, NY)),
            dma((2,)),
            dma((2, 8)),
            dma((2,)),
            dma((8,)),
            dma((2, 4)),
            dma((2, 4)),
            dma((2, 4)),
            dma((2, 4, NY)),
            dma((3,)),
            dma((3,)),
            dma,
            dma,
        ],
        compiler_params=pltpu.CompilerParams(
            collective_id=0, has_side_effects=True, vmem_limit_bytes=60 * 2**20
        ),
        cost_estimate=pl.CostEstimate(flops=10**10, bytes_accessed=12 * 10**6, transcendentals=LIVE * FF),
        name="swiglu",
    )(counts, tv, ts, gv, gs.T, uv, us.T, dv, ds.T)


def solution(mesh):
    rows, split = P(("replica", "group"), None), P("group", None)
    in_specs = (rows, rows, P("replica")) + (split,) * 6
    return jax.shard_map(shards, mesh=mesh, in_specs=in_specs, out_specs=rows, check_vma=False)
```

time: 151 us -> 145 us (0.960)
  Pallas kernels: 148 us -> 143 us
    pallas_call x1, Pallas kernels: 148 us -> 143 us  [shards(): pl.pallas_call(kernel, out_shape=jax.ShapeDtypeStruct((CAP, DO), BF16), i...]
where the time goes in v3:
time: 145 us; the launch traced here: 144 us
  Pallas kernels  143 us (99%)
  local copies, waits for them, and re-layouts  1.69 us (1%)
    pallas_call x1, Pallas kernels, shards(): pl.pallas_call(kernel, out_shape=jax.ShapeDtypeStruct((CAP, DO), BF16), i...  143 us

profile of v3, /device:TPU:4, one launch (start us, length us, event | category | flops | bytes accessed | tf_op | source)
XLA Modules:
  0.0 144.4 jit_solution(13513164407130195075)
XLA Ops:
  0.0 142.7 %swiglu.1 = bf16[40,3584]{1,0:T(8,128)(2,1)} custom-call(s32[32]{0:T(128)} %counts.1, bf16[40,7168]{1,0:T(8,128)(2,1)} %tv_h.1, bf16[40,56]{1,0:T(8,128)(2,1)} %ts_h.1, bf16[288,7168]{1,0:T(8,128)(2,1)} %gv_h.1, f32[56,288]{1,0:T(8,128)} %bitcast.3, bf16[288,7168]{1,0:T(8,128)(2,1)} %uv_h.1, f32[56,288]{1,0:T(8,128)} %bitcast.4, bf16[288,3584]{1,0:T(8,128)(2,1)} %dv_h.1, ...), custom_call_target="tpu_custom_call" | custom-call | flops 10000000000 | bytes 12000000 | tf_op jit(solution)/shard_map/swiglu/pallas_call | solution.py:546
  142.7 1.7 %copy.11 = bf16[40,3584]{1,0:T(8,128)(2,1)} copy(bf16[40,3584]{1,0:T(8,128)(2,1)} %swiglu.1) | data formatting | bytes 573440

commit v4 on v3

--- a/solution.py
+++ b/solution.py
@@ -45,14 +45,14 @@
 )
 
 SUMS = (
-    ("tz", 0, 3, 1), ("tz", 1, 3, 0), ("ya", 1, 4), ("tz", 0, 3, 0), ("tz", 0, 3, 3), ("tz", 1, 3, 1),
-    ("tz", 1, 3, 2), ("tz", 0, 3, 2), ("ya", 1, -3), ("ya", 0, 4), ("ya", 1, 3), ("tz", 0, 2, 1), ("ya", 0, -3),
-    ("tz", 1, 3, 3), ("tz", 0, 2, 0), ("ya", 0, 3), ("ya", 0, -2), ("tz", 1, 2, 0), ("tz", 0, 2, 3), ("ya", 1, -2),
-    ("tz", 1, 2, 2), ("ya", 0, 2), ("line", 4), ("tz", 0, 2, 2), ("tz", 1, 2, 1), ("ya", 1, 2), ("ya", 0, 1),
-    ("tz", 0, 1, 0), ("ya", 1, -1), ("tz", 1, 2, 3), ("line", -3), ("line", 3), ("tz", 1, 1, 2), ("tz", 0, 1, 2),
-    ("ya", 0, 0), ("ya", 1, 0), ("ya", 0, -1), ("tz", 0, 1, 3), ("tz", 1, 1, 3), ("ya", 1, 1), ("line", -2),
-    ("line", 2), ("tz", 1, 1, 1), ("tz", 0, 1, 1), ("tz0", 3), ("tz", 1, 1, 0), ("tz0", 2), ("line", -1), ("line", 1),
-    ("tz0", 1), ("tz0", 0), ("line", 0), ("fin",),
+    ("tz", 1, 3, 1), ("tz", 0, 3, 1), ("tz", 0, 3, 2), ("tz", 1, 3, 2), ("tz", 1, 3, 3), ("ya", 1, 4), ("ya", 0, 4),
+    ("tz", 1, 3, 0), ("tz", 0, 3, 0), ("tz", 0, 3, 3), ("ya", 0, 3), ("ya", 0, -3), ("tz", 1, 2, 1), ("tz", 0, 2, 1),
+    ("tz", 0, 2, 2), ("ya", 1, -3), ("ya", 1, 3), ("ya", 1, -2), ("tz", 1, 2, 2), ("tz", 0, 2, 0), ("tz", 1, 2, 3),
+    ("line", 4), ("tz", 1, 2, 0), ("ya", 1, 2), ("ya", 0, 2), ("tz", 0, 2, 3), ("tz", 0, 1, 2), ("tz", 1, 1, 2),
+    ("ya", 0, -2), ("line", 3), ("line", -3), ("ya", 1, -1), ("tz", 0, 1, 3), ("tz", 1, 1, 1), ("tz", 0, 1, 1),
+    ("ya", 1, 1), ("ya", 0, -1), ("ya", 0, 1), ("tz0", 2), ("tz", 1, 1, 3), ("ya", 1, 0), ("line", 2), ("line", -2),
+    ("tz", 1, 1, 0), ("ya", 0, 0), ("tz", 0, 1, 0), ("tz0", 3), ("tz0", 1), ("line", 1), ("line", -1), ("tz0", 0),
+    ("fin",), ("line", 0),
 )
 
 
@@ -322,38 +322,6 @@
             return c
 
         lax.fori_loop(0, NY if d in (0, 4) else 2 * NY, body, 0)
-
-    @pl.when(is_holder)
-    def _():
-        for h in range(2):
-            ring[mine, pl.ds(h * HALF, HALF), :] = jnp.dot(
-                onehot[pl.ds(h * HALF, HALF), :], xs[...], preferred_element_type=F32
-            ).astype(BF16)
-        for way in range(2):
-            y2(way, 0, mine).start()
-        for i in range(2):
-            for way in range(2):
-                z1(way, 0, i if way == 0 else 1 - i, mine).start()
-
-    y1_send(0, 0)
-    y1_send(0, 1)
-    z2_send(0)
-    for n, (wave, *which) in enumerate(ARRIVALS):
-        takes[wave](*which)
-        later = ARRIVALS[n + 1 :]
-        if wave == "z2" and not any(o[0] == "z2" and o[2] == which[1] for o in later):
-            ring_of(which[1] + 1)
-        if wave == "y2" and not any(o[0] == "y2" for o in later):
-            ring_of(0)
-        if wave == "y1" and not any(o[0] == "y1" and o[2] == which[1] for o in later):
-            column(which[1], 3 if which[1] == 4 else 0, 4)
-        if wave == "y1" and which[1:3] == [4, 0] and not any(o[0] == "y1" and o[2:4] == (4, 0) for o in later):
-            column(4, 0, 3)
-
-    for r in range(LIVE // 128):
-        rows = pl.ds(r * 128, 128)
-        gate = acc[rows, 0:FP]
-        hid[rows, :] = (gate / (1.0 + jnp.exp(-gate)) * acc[rows, FP : 2 * FP]).astype(BF16)
 
     def slab(dy):
         yy = (y + dy) % NY
@@ -468,15 +436,54 @@
         when(0, 0, f)
 
     sums = {"ya": sum_ya, "line": sum_line, "tz": sum_tz, "tz0": sum_tz0, "fin": sum_fin}
-    for dy in range(NY):
-        slab_far(dy)
-    for dy in range(NY):
-
-        def f(p, dy=dy):
-            mt(0, 4, dy, p).start()
-            mt(1, 4, dy, p).start()
-
-        when(4, dy, f)
+    def hidden(lo, hi):
+        for r in range(lo, hi, 64):
+            rows = pl.ds(r, 64)
+            gate = acc[rows, 0:FP]
+            hid[rows, :] = (gate / (1.0 + jnp.exp(-gate)) * acc[rows, FP : 2 * FP]).astype(BF16)
+
+    def start_far():
+        for dy in range(NY):
+            slab_far(dy)
+        for dy in range(NY):
+
+            def f(p, dy=dy):
+                mt(0, 4, dy, p).start()
+                mt(1, 4, dy, p).start()
+
+            when(4, dy, f)
+
+    @pl.when(is_holder)
+    def _():
+        for h in range(2):
+            ring[mine, pl.ds(h * HALF, HALF), :] = jnp.dot(
+                onehot[pl.ds(h * HALF, HALF), :], xs[...], preferred_element_type=F32
+            ).astype(BF16)
+        for way in range(2):
+            y2(way, 0, mine).start()
+        for i in range(2):
+            for way in range(2):
+                z1(way, 0, i if way == 0 else 1 - i, mine).start()
+
+    y1_send(0, 0)
+    y1_send(0, 1)
+    z2_send(0)
+    for n, (wave, *which) in enumerate(ARRIVALS):
+        takes[wave](*which)
+        later = ARRIVALS[n + 1 :]
+        if wave == "z2" and not any(o[0] == "z2" and o[2] == which[1] for o in later):
+            ring_of(which[1] + 1)
+            if which[1] == 3:
+                hidden(T1, LIVE)
+                start_far()
+        if wave == "y2" and not any(o[0] == "y2" for o in later):
+            ring_of(0)
+        if wave == "y1" and not any(o[0] == "y1" and o[2] == which[1] for o in later):
+            column(which[1], 3 if which[1] == 4 else 0, 4)
+        if wave == "y1" and which[1:3] == [4, 0] and not any(o[0] == "y1" and o[2:4] == (4, 0) for o in later):
+            column(4, 0, 3)
+
+    hidden(0, T1)
     slab(2)
     for e in ORDER:
 

time: 145 us -> 146 us (level)
  no operation moved by 1% of the time
where the time goes in v4:
time: 146 us
  Pallas kernels  144 us (99%)
  local copies, waits for them, and re-layouts  1.69 us (1%)
    pallas_call x1, Pallas kernels, shards(): pl.pallas_call(kernel, out_shape=jax.ShapeDtypeStruct((CAP, DO), BF16), i...  144 us

profile of v4, /device:TPU:4, one launch (start us, length us, event | category | flops | bytes accessed | tf_op | source)
XLA Modules:
  0.0 145.7 jit_solution(4604699272555514779)
XLA Ops:
  0.0 144.0 %swiglu.1 = bf16[40,3584]{1,0:T(8,128)(2,1)} custom-call(s32[32]{0:T(128)} %counts.1, bf16[40,7168]{1,0:T(8,128)(2,1)} %tv_h.1, bf16[40,56]{1,0:T(8,128)(2,1)} %ts_h.1, bf16[288,7168]{1,0:T(8,128)(2,1)} %gv_h.1, f32[56,288]{1,0:T(8,128)} %bitcast.3, bf16[288,7168]{1,0:T(8,128)(2,1)} %uv_h.1, f32[56,288]{1,0:T(8,128)} %bitcast.4, bf16[288,3584]{1,0:T(8,128)(2,1)} %dv_h.1, ...), custom_call_target="tpu_custom_call" | custom-call | flops 10000000000 | bytes 12000000 | tf_op jit(solution)/shard_map/swiglu/pallas_call | solution.py:553
  144.0 1.7 %copy.11 = bf16[40,3584]{1,0:T(8,128)(2,1)} copy(bf16[40,3584]{1,0:T(8,128)(2,1)} %swiglu.1) | data formatting | bytes 573440
